TPU v7x, 32 devices: a whole 2x2x4 slice. The times are simulated.
32 devices in a mesh: dp: 8 (over z, x), tensor: 4 (over y, core).
Axes of the slice: x: 2, y: 2, z: 4, core: 2. Of those that a mesh axis runs over, the one named last changes fastest.
Arguments:
- inputs: bfloat16 [2, 6144, 768], P(None, 'dp'), may hold values from -6 to 6
- time_first: bfloat16 [8, 13, 768], P('dp'), may hold values from -6 to 6
- time_second: bfloat16 [8, 7, 768], P('dp'), may hold values from -6 to 6
- lengths_first: int32 [8, 13], P('dp'), may hold values from 1 to 64, 720 in all within a row
- lengths_second: int32 [8, 7], P('dp'), may hold values from 1 to 128, 720 in all within a row
- cotangent: bfloat16 [2, 6144, 768], P(None, 'dp'), may hold values from -6 to 6
- w_qkv: float32 [768, 3, 768], P('dp', None, 'tensor'), may hold values from -0.21875 to 0.21875
- m_qkv: float32 [768, 3, 768], P('dp', None, 'tensor'), may hold values from -0.0078125 to 0.0078125
- v_qkv: float32 [768, 3, 768], P('dp', None, 'tensor'), may hold values from 2.7126737e-07 to 1.0850695e-06
- w_proj: float32 [768, 768], P('tensor', 'dp'), may hold values from -1.75 to 1.75
- m_proj: float32 [768, 768], P('tensor', 'dp'), may hold values from -0.0012207031 to 0.0012207031
- v_proj: float32 [768, 768], P('tensor', 'dp'), may hold values from 6.1035155e-09 to 2.4414062e-08
- w_up: float32 [768, 3072], P('dp', 'tensor'), may hold values from -0.21875 to 0.21875
- m_up: float32 [768, 3072], P('dp', 'tensor'), may hold values from -0.0029296875 to 0.0029296875
- v_up: float32 [768, 3072], P('dp', 'tensor'), may hold values from 3.8146972e-08 to 1.5258789e-07
- w_down: float32 [3072, 768], P('tensor', 'dp'), may hold values from -0.109375 to 0.109375
- m_down: float32 [3072, 768], P('tensor', 'dp'), may hold values from -0.0048828125 to 0.0048828125
- v_down: float32 [3072, 768], P('tensor', 'dp'), may hold values from 1.235962e-07 to 4.943848e-07
- w_vecs: float32 [6, 768], replicated, may hold values from -0.3 to 1.2
- m_vecs: float32 [6, 768], replicated, may hold values from -0.009765625 to 0.009765625
- v_vecs: float32 [6, 768], replicated, may hold values from 4.2385525e-07 to 1.695421e-06
- b_heads: float32 [2, 768], P(None, 'tensor'), may hold values from -4 to 4
- m_heads: float32 [2, 768], P(None, 'tensor'), may hold values from -0.0078125 to 0.0078125
- v_heads: float32 [2, 768], P(None, 'tensor'), may hold values from 3.4332277e-07 to 1.3732911e-06
- b_hidden: float32 [3072], P('tensor'), may hold values from -4 to 4
- m_hidden: float32 [3072], P('tensor'), may hold values from -0.0024414062 to 0.0024414062
- v_hidden: float32 [3072], P('tensor'), may hold values from 3.323025e-08 to 1.32921e-07
Outputs:
- block_out: bfloat16 [2, 6144, 768], P(None, 'dp')
- input_grad: float32 [2, 6144, 768], P(None, 'dp')
- grad_norm: float32 [1], replicated
- stream_rms: float32 [3], replicated
- qkv_next: float32 [768, 3, 768], P('dp', None, 'tensor')
- qkv_moment: float32 [768, 3, 768], P('dp', None, 'tensor')
- qkv_square: float32 [768, 3, 768], P('dp', None, 'tensor')
- proj_next: float32 [768, 768], P('tensor', 'dp')
- proj_moment: float32 [768, 768], P('tensor', 'dp')
- proj_square: float32 [768, 768], P('tensor', 'dp')
- up_next: float32 [768, 3072], P('dp', 'tensor')
- up_moment: float32 [768, 3072], P('dp', 'tensor')
- up_square: float32 [768, 3072], P('dp', 'tensor')
- down_next: float32 [3072, 768], P('tensor', 'dp')
- down_moment: float32 [3072, 768], P('tensor', 'dp')
- down_square: float32 [3072, 768], P('tensor', 'dp')
- vecs_next: float32 [6, 768], replicated
- vecs_moment: float32 [6, 768], replicated
- vecs_square: float32 [6, 768], replicated
- heads_next: float32 [2, 768], P(None, 'tensor')
- heads_moment: float32 [2, 768], P(None, 'tensor')
- heads_square: float32 [2, 768], P(None, 'tensor')
- hidden_next: float32 [3072], P('tensor')
- hidden_moment: float32 [3072], P('tensor')
- hidden_square: float32 [3072], P('tensor')
Inputs may be any that keep to these rules, and one draw needn't show every extreme that they name: `lengths_first`: each row sums to 720 and its longest entry is exactly 64. `lengths_second`: each row sums to 720 and its longest entry is exactly 128.
All inputs are finite; a program needn't handle non-finite values.
Results may differ from a plain program's by a relative error of at most 0.008.
The roundings to bfloat16 on the way count: a program that leaves them out, or rounds other values in their place, can miss the bound.
Values may be sent and summed in bfloat16 or wider, within the bound.
No kernel may reach another device: no remote copies, remote signals or barrier semaphores. Data moves between devices by JAX's collectives and lax.ppermute only.
A program may use at most 128 MiB of HBM per device.

v0:
```python
from functools import partial

import jax
import jax.numpy as jnp
from jax import lax
from jax.sharding import PartitionSpec as P

HD = 64
STEP = 5


norm_eps = 1e-05
clip_limit = 1.0
beta_first = 0.5
beta_second = 0.5
adam_eps = 1e-08
matrix_decay = 0.01
masked_score = -1e30
step_rates = (0.03, 0.2, 0.03, 0.015, 0.3, 0.3, 0.3)


def layer_norm(stream, gain_row, offset_row):
    center = stream - jnp.mean(stream, axis=-1, keepdims=True)
    spread = jnp.mean(center * center, axis=-1, keepdims=True)
    return center * lax.rsqrt(spread + norm_eps) * gain_row + offset_row


def exact_gelu(values_in):
    return jax.nn.gelu(values_in, approximate=False)


def segment_ids(lengths_row, rows_count, first_id):
    bounds = jnp.cumsum(lengths_row)
    places = jnp.arange(rows_count, dtype=jnp.int32)
    return first_id + jnp.sum((places[:, None] >= bounds[None, :]).astype(jnp.int32), axis=1)


def adamw_step(
    weight,
    moment_old,
    square_old,
    gradient,
    step_rate,
    decay_value,
    clip_factor,
    correct_one,
    correct_two,
):
    clipped = gradient * clip_factor
    moment_new = beta_first * moment_old + (1.0 - beta_first) * clipped
    square_new = beta_second * square_old + (1.0 - beta_second) * clipped * clipped
    divisor = jnp.sqrt(square_new / correct_two) + adam_eps
    weight_new = weight - step_rate * (moment_new / correct_one / divisor + decay_value * weight)
    return (weight_new, moment_new, square_new)


def local(
    inputs,
    time_first,
    time_second,
    lengths_first,
    lengths_second,
    cotangent,
    w_qkv,
    m_qkv,
    v_qkv,
    w_proj,
    m_proj,
    v_proj,
    w_up,
    m_up,
    v_up,
    w_down,
    m_down,
    v_down,
    w_vecs,
    m_vecs,
    v_vecs,
    b_heads,
    m_heads,
    v_heads,
    b_hidden,
    m_hidden,
    v_hidden,
):
    batch_rows = inputs.shape[1]
    features = inputs.shape[2]
    all_rows = 2 * batch_rows
    seqs_first = time_first.shape[1]
    seqs_second = time_second.shape[1]
    full_qkv, full_proj, full_up, full_down = (
        lax.all_gather(w_qkv.astype(jnp.bfloat16), "dp", axis=0, tiled=True),
        lax.all_gather(w_proj.astype(jnp.bfloat16), "dp", axis=1, tiled=True),
        lax.all_gather(w_up.astype(jnp.bfloat16), "dp", axis=0, tiled=True),
        lax.all_gather(w_down.astype(jnp.bfloat16), "dp", axis=1, tiled=True),
    )
    local_width = full_qkv.shape[2]
    heads_local = local_width // HD
    qkv_matrix = full_qkv.reshape(features, 3 * local_width)
    ids_first = segment_ids(lengths_first[0], batch_rows, 0)
    ids_second = segment_ids(lengths_second[0], batch_rows, seqs_first + 1)
    segments = jnp.concatenate([ids_first, ids_second])
    valid_rows = jnp.concatenate(
        [ids_first < seqs_first, ids_second < seqs_first + 1 + seqs_second]
    ).astype(jnp.float32)[:, None]
    pick_first = (ids_first[:, None] == jnp.arange(seqs_first, dtype=jnp.int32)[None, :]).astype(
        jnp.bfloat16
    )
    pick_second = (
        ids_second[:, None] == seqs_first + 1 + jnp.arange(seqs_second, dtype=jnp.int32)[None, :]
    ).astype(jnp.bfloat16)
    time_rows = jnp.concatenate(
        [
            jnp.dot(pick_first, time_first[0], preferred_element_type=jnp.float32),
            jnp.dot(pick_second, time_second[0], preferred_element_type=jnp.float32),
        ]
    )
    stream = inputs.reshape(all_rows, features).astype(jnp.float32) + time_rows
    upstream = cotangent.reshape(all_rows, features).astype(jnp.float32) * valid_rows
    normed_full, norm_one_back = jax.vjp(layer_norm, stream, w_vecs[0], w_vecs[1])
    normed = normed_full.astype(jnp.bfloat16)
    mixed_all = jnp.dot(normed, qkv_matrix, preferred_element_type=jnp.float32)
    queries = (mixed_all[:, :local_width] + b_heads[0]).astype(jnp.bfloat16)
    keyset = mixed_all[:, local_width : 2 * local_width].astype(jnp.bfloat16)
    valueset = (mixed_all[:, 2 * local_width :] + b_heads[1]).astype(jnp.bfloat16)
    scaling = HD ** (-0.5)
    half_shape = (2, batch_rows, heads_local, HD)
    query_halves = queries.reshape(half_shape)
    key_halves = keyset.reshape(half_shape)
    value_halves = valueset.reshape(half_shape)
    segment_halves = segments.reshape(2, batch_rows)

    def half_scores(query_half, key_half, segment_half):
        scores = (
            jnp.einsum("qhc,khc->hqk", query_half, key_half, preferred_element_type=jnp.float32)
            * scaling
        )
        allowed = segment_half[:, None] == segment_half[None, :]
        return jnp.where(allowed[None], scores, masked_score)

    def attend_forward(pieces):
        query_half, key_half, value_half, segment_half = pieces
        scores = half_scores(query_half, key_half, segment_half)
        peak_rows = jnp.max(scores, axis=-1, keepdims=True)
        exponent = jnp.exp(scores - peak_rows)
        totals = jnp.sum(exponent, axis=-1, keepdims=True)
        probs_low = (exponent / totals).astype(jnp.bfloat16)
        result = jnp.einsum(
            "hqk,khc->qhc", probs_low, value_half, preferred_element_type=jnp.float32
        )
        return (result.astype(jnp.bfloat16), (peak_rows + jnp.log(totals))[..., 0])

    attended_halves, lse_halves = lax.map(
        attend_forward, (query_halves, key_halves, value_halves, segment_halves)
    )
    attended = attended_halves.reshape(all_rows, local_width)
    branch_rows = (
        lax.psum(jnp.dot(attended, full_proj, preferred_element_type=jnp.float32), "tensor")
        + w_vecs[4]
    )
    middle_rows = stream + branch_rows
    normed_two_rows, norm_two_back = jax.vjp(layer_norm, middle_rows, w_vecs[2], w_vecs[3])
    normed_two = normed_two_rows.astype(jnp.bfloat16)
    hidden = jnp.dot(normed_two, full_up, preferred_element_type=jnp.float32) + b_hidden
    active_full, gelu_back = jax.vjp(exact_gelu, hidden)
    active = active_full.astype(jnp.bfloat16)
    branch_two_rows = (
        lax.psum(
            jnp.dot(active, full_down, preferred_element_type=jnp.float32).astype(jnp.bfloat16),
            "tensor",
        ).astype(jnp.float32)
        + w_vecs[5]
    )
    sum_rows = middle_rows + branch_two_rows
    out_low = sum_rows.astype(jnp.bfloat16)
    upstream_low = upstream.astype(jnp.bfloat16)
    grad_down = jnp.einsum("rf,rd->fd", active, upstream_low, preferred_element_type=jnp.float32)
    grad_active = jnp.einsum(
        "rd,fd->rf", upstream_low, full_down, preferred_element_type=jnp.float32
    )
    (grad_hidden,) = gelu_back(grad_active)
    grad_hidden_low = grad_hidden.astype(jnp.bfloat16)
    grad_up = jnp.einsum(
        "rd,rf->df", normed_two, grad_hidden_low, preferred_element_type=jnp.float32
    )
    grad_normed_two = lax.psum(
        jnp.einsum("rf,df->rd", grad_hidden_low, full_up, preferred_element_type=jnp.float32),
        "tensor",
    )
    grad_middle_norm, grad_gain_two, grad_offset_two = norm_two_back(grad_normed_two)
    grad_middle_rows = upstream + grad_middle_norm
    middle_low_rows = grad_middle_rows.astype(jnp.bfloat16)
    grad_proj = jnp.einsum(
        "rc,rd->cd", attended, middle_low_rows, preferred_element_type=jnp.float32
    )
    grad_attended = jnp.einsum(
        "rd,cd->rc", middle_low_rows, full_proj, preferred_element_type=jnp.float32
    ).astype(jnp.bfloat16)
    grad_halves = grad_attended.reshape(half_shape)

    def attend_backward(pieces):
        query_half, key_half, value_half, segment_half, lse_half, grad_half = pieces
        scores = half_scores(query_half, key_half, segment_half)
        probs = jnp.exp(scores - lse_half[..., None])
        probs_low = probs.astype(jnp.bfloat16)
        grad_probs = jnp.einsum(
            "qhc,khc->hqk", grad_half, value_half, preferred_element_type=jnp.float32
        )
        grad_value = jnp.einsum(
            "hqk,qhc->khc", probs_low, grad_half, preferred_element_type=jnp.float32
        )
        inner_sum = jnp.sum(probs * grad_probs, axis=-1, keepdims=True)
        grad_scores = (probs * (grad_probs - inner_sum)).astype(jnp.bfloat16)
        grad_query = (
            jnp.einsum("hqk,khc->qhc", grad_scores, key_half, preferred_element_type=jnp.float32)
            * scaling
        )
        grad_key = (
            jnp.einsum("hqk,qhc->khc", grad_scores, query_half, preferred_element_type=jnp.float32)
            * scaling
        )
        return (
            grad_query.astype(jnp.bfloat16),
            grad_key.astype(jnp.bfloat16),
            grad_value.astype(jnp.bfloat16),
        )

    query_grads, key_grads, value_grads = lax.map(
        attend_backward,
        (query_halves, key_halves, value_halves, segment_halves, lse_halves, grad_halves),
    )
    grad_queries = query_grads.reshape(all_rows, local_width)
    grad_keys = key_grads.reshape(all_rows, local_width)
    grad_values = value_grads.reshape(all_rows, local_width)
    grad_mixed = jnp.concatenate([grad_queries, grad_keys, grad_values], axis=1)
    grad_qkv = jnp.einsum(
        "rd,rj->dj", normed, grad_mixed, preferred_element_type=jnp.float32
    ).reshape(features, 3, local_width)
    grad_normed = lax.psum(
        jnp.einsum("rj,dj->rd", grad_mixed, qkv_matrix, preferred_element_type=jnp.float32),
        "tensor",
    )
    grad_stream_norm, grad_gain_one, grad_offset_one = norm_one_back(grad_normed)
    input_rows = grad_middle_rows + grad_stream_norm
    vec_part = jnp.stack(
        [
            grad_gain_one,
            grad_offset_one,
            grad_gain_two,
            grad_offset_two,
            jnp.sum(grad_middle_rows, axis=0),
            jnp.sum(upstream, axis=0),
        ]
    )
    square_part = jnp.stack(
        [
            jnp.sum(valid_rows * sum_rows * sum_rows),
            jnp.sum(valid_rows * branch_rows * branch_rows),
            jnp.sum(valid_rows * branch_two_rows * branch_two_rows),
        ]
    )
    input_grad = input_rows.reshape(2, batch_rows, features)
    grad_heads = jnp.stack(
        [
            jnp.sum(grad_queries, axis=0, dtype=jnp.float32),
            jnp.sum(grad_values, axis=0, dtype=jnp.float32),
        ]
    )
    grad_offsets = jnp.sum(grad_hidden, axis=0)
    valid_count = jnp.sum(valid_rows)
    dp_index = lax.axis_index("dp")
    tensor_first = (lax.axis_index("tensor") == 0).astype(jnp.float32)
    rows_qkv = w_qkv.shape[0]
    cols_proj = w_proj.shape[1]
    rows_up = w_up.shape[0]
    cols_down = w_down.shape[1]
    summed = lax.psum(
        (
            grad_qkv,
            grad_proj,
            grad_up,
            grad_down,
            vec_part,
            grad_heads,
            grad_offsets,
            square_part,
            valid_count,
        ),
        "dp",
    )
    sum_qkv, sum_proj, sum_up, sum_down, sum_vecs, sum_heads, sum_hidden, sum_squares, sum_count = (
        summed
    )
    partial_square = (
        jnp.sum(sum_qkv * sum_qkv)
        + jnp.sum(sum_proj * sum_proj)
        + jnp.sum(sum_up * sum_up)
        + jnp.sum(sum_down * sum_down)
        + jnp.sum(sum_heads * sum_heads)
        + jnp.sum(sum_hidden * sum_hidden)
        + tensor_first * jnp.sum(sum_vecs * sum_vecs)
    )
    total_square = lax.psum(partial_square, "tensor")
    own_qkv = lax.dynamic_slice_in_dim(sum_qkv, dp_index * rows_qkv, rows_qkv, 0)
    own_proj = lax.dynamic_slice_in_dim(sum_proj, dp_index * cols_proj, cols_proj, 1)
    own_up = lax.dynamic_slice_in_dim(sum_up, dp_index * rows_up, rows_up, 0)
    own_down = lax.dynamic_slice_in_dim(sum_down, dp_index * cols_down, cols_down, 1)
    grad_norm = jnp.sqrt(total_square)
    clip_factor = jnp.minimum(1.0, clip_limit / (grad_norm + 1e-06))
    correct_one = 1.0 - beta_first**STEP
    correct_two = 1.0 - beta_second**STEP
    update = partial(
        adamw_step, clip_factor=clip_factor, correct_one=correct_one, correct_two=correct_two
    )
    qkv_next, qkv_moment, qkv_square = update(
        w_qkv, m_qkv, v_qkv, own_qkv, step_rates[0], matrix_decay
    )
    proj_next, proj_moment, proj_square = update(
        w_proj, m_proj, v_proj, own_proj, step_rates[1], matrix_decay
    )
    up_next, up_moment, up_square = update(w_up, m_up, v_up, own_up, step_rates[2], matrix_decay)
    down_next, down_moment, down_square = update(
        w_down, m_down, v_down, own_down, step_rates[3], matrix_decay
    )
    vecs_next, vecs_moment, vecs_square = update(
        w_vecs, m_vecs, v_vecs, sum_vecs, step_rates[4], 0.0
    )
    heads_next, heads_moment, heads_square = update(
        b_heads, m_heads, v_heads, sum_heads, step_rates[5], 0.0
    )
    hidden_next, hidden_moment, hidden_square = update(
        b_hidden, m_hidden, v_hidden, sum_hidden, step_rates[6], 0.0
    )
    stream_rms = jnp.sqrt(sum_squares / (sum_count * features))
    block_out = out_low.reshape(2, batch_rows, features)
    return (
        block_out,
        input_grad,
        grad_norm.reshape(1),
        stream_rms,
        qkv_next,
        qkv_moment,
        qkv_square,
        proj_next,
        proj_moment,
        proj_square,
        up_next,
        up_moment,
        up_square,
        down_next,
        down_moment,
        down_square,
        vecs_next,
        vecs_moment,
        vecs_square,
        heads_next,
        heads_moment,
        heads_square,
        hidden_next,
        hidden_moment,
        hidden_square,
    )


def solution(mesh):
    return jax.shard_map(
        local,
        mesh=mesh,
        in_specs=(
            P(None, "dp", None),
            P("dp", None, None),
            P("dp", None, None),
            P("dp", None),
            P("dp", None),
            P(None, "dp", None),
            P("dp", None, "tensor"),
            P("dp", None, "tensor"),
            P("dp", None, "tensor"),
            P("tensor", "dp"),
            P("tensor", "dp"),
            P("tensor", "dp"),
            P("dp", "tensor"),
            P("dp", "tensor"),
            P("dp", "tensor"),
            P("tensor", "dp"),
            P("tensor", "dp"),
            P("tensor", "dp"),
            P(),
            P(),
            P(),
            P(None, "tensor"),
            P(None, "tensor"),
            P(None, "tensor"),
            P("tensor"),
            P("tensor"),
            P("tensor"),
        ),
        out_specs=(
            P(None, "dp", None),
            P(None, "dp", None),
            P(),
            P(),
            P("dp", None, "tensor"),
            P("dp", None, "tensor"),
            P("dp", None, "tensor"),
            P("tensor", "dp"),
            P("tensor", "dp"),
            P("tensor", "dp"),
            P("dp", "tensor"),
            P("dp", "tensor"),
            P("dp", "tensor"),
            P("tensor", "dp"),
            P("tensor", "dp"),
            P("tensor", "dp"),
            P(),
            P(),
            P(),
            P(None, "tensor"),
            P(None, "tensor"),
            P(None, "tensor"),
            P("tensor"),
            P("tensor"),
            P("tensor"),
        ),
        check_vma=False,
    )
```

profile of v0, /device:TPU:0, one launch (start us, length us, event | category | flops | bytes accessed | tf_op | source)
XLA Modules:
  0.0 848.0 jit_solution(16327075515374586013)
XLA Ops:
  10.8 1.6 slice_reduce_fusion
  14.5 33.2 %all_gather.13 = bf16[192,768]{0,1:T(8,128)(2,1)S(1)} all-gather(bf16[192,96]{0,1:T(8,128)(2,1)S(1)} %copy.181), channel_id=1, replica_groups=mesh['dp'=8,'tensor'=4] {'dp'}, dimensions={1}, use_global_device_ids=true | all-gather | bytes 331776 | tf_op jit(solution)/shard_map/all_gather | solution.py:93
  47.7 39.1 %all_gather.12 = bf16[768,3,192]{2,1,0:T(4,128)(2,1)S(1)} all-gather(bf16[96,3,192]{2,1,0:T(4,128)(2,1)S(1)} %copy.175), channel_id=1, replica_groups=mesh['dp'=8,'tensor'=4] {'dp'}, dimensions={0}, use_global_device_ids=true | all-gather | bytes 995328 | tf_op jit(solution)/shard_map/all_gather | solution.py:92
  86.8 2.1 copy.176
  96.3 1.6 fusion.114
  101.8 2.7 reshape.434
  104.5 2.0 copy.179
  106.4 2.6 reshape.431
  109.1 1.9 copy.177
  111.9 15.8 %while.26 = (s32[]{:T(128)}, bf16[2,768,3,64]{1,3,2,0:T(8,128)(2,1)}, f32[2,3,768]{2,1,0:T(4,128)S(1)}, bf16[2,768,3,64]{1,3,2,0:T(8,128)(2,1)}, s32[2,768]{1,0:...) while((s32[]{:T(128)}, ...), condition=%wide.region_9.10_spmd, body=%wide.region_6.9_spmd.sunk | while | flops 474953472 | bytes 31951032 | solution.py:153
  112.3 2.4 fusion.161
  116.3 2.5 fusion.163
  120.0 2.4 fusion.161
  122.5 1.5 fusion.162
  124.1 2.5 fusion.163
  127.6 1.7 copy.180
  130.2 3.0 fusion.115
  133.3 1.6 convert_element_type.155
  135.0 1.6 convert_element_type.157
  136.8 3.7 fusion.69
  140.4 88.1 %all-reduce.8.cloned.1.call-done = f32[1536,768]{1,0:T(8,128)} async-done(((f32[1536,768]{1,0:T(8,128)}), f32[1536,768]{1,0:T(8,128)}) %all-reduce.8.cloned.1.call-update) | async-done | bytes 4718608 | tf_op jit(solution)/shard_map/psum | solution.py:158
  228.5 4.8 fusion.112
  236.6 6.4 fusion.116
  243.0 14.5 %fusion.108 = (f32[768]{0:T(1024)S(1)}, bf16[1536,768]{1,0:T(8,128)(2,1)S(1)}, f32[1536,768]{1,0:T(8,128)S(1)}) fusion(f32[1536,768]{1,0:T(8,128)} %fusion.116, f32[768]{0:T(1024)S(1)} %copy-done.53, bf16[1536,768]{1,0:T(8,128)(2,1)} %fusion.69, bf16[768,768]{0,1:T(8,128)(2,1)} %all-gather.5.cloned.1.call-done), kind=kOutput, calls=%fused_computation.212 | convolution fusion | flops 1899232512 | bytes 15341568 | tf_op jit(solution)/shard_map/rd,fd->rf/dot_general | solution.py:178
  259.8 3.5 convolution_convert_fusion
  263.3 9.7 %all-reduce.12.cloned.1.call-start = ((), (), s32[]{:S(2)}) async-start(), calls=%async_computation.4 | async-start | bytes 9437184 | tf_op jit(solution)/shard_map/psum | solution.py:186
  272.9 5.6 fusion.79
  278.6 40.6 %all-reduce.10.cloned.1.call-done = bf16[1536,768]{1,0:T(8,128)(2,1)} async-done(((bf16[1536,768]{1,0:T(8,128)(2,1)}), bf16[1536,768]{1,0:T(8,128)(2,1)}) %all-reduce.10.cloned.1.call-update) | async-done | bytes 2359312 | tf_op jit(solution)/shard_map/psum | solution.py:168
  319.2 97.1 %all-reduce.12.cloned.1.call-done = f32[1536,768]{1,0:T(8,128)} async-done(((f32[1536,768]{1,0:T(8,128)}), f32[1536,768]{1,0:T(8,128)}) %all-reduce.12.cloned.1.call-update) | async-done | bytes 4718608 | tf_op jit(solution)/shard_map/psum | solution.py:186
  416.3 11.4 %fusion.61 = (f32[]{:T(128)}, f32[]{:T(128)}, bf16[1536,768]{1,0:T(8,128)(2,1)}, f32[768]{0:T(1024)S(1)}, f32[]{:T(128)}, /*index=5*/f32[1536]{0:T(1024)S(1)}, f32[768]{0:T(1024)S(1)}) fusion(f32[1536,768]{1,0:T(8,128)} %all-reduce.8.cloned.1.call-done, f32[1536]{0:T(1024)S(1)} %add_convert_fusion.3, f32[768]{0:T(1024)S(1)} %get-tuple-element.342, ...), kind=kLoop, calls=%fused_computation.74 | loop fusion | flops 25949180 | bytes 18914316 | tf_op jit(solution)/shard_map/reduce_sum | solution.py:258
  427.7 2.2 fusion.111
  431.0 2.2 copy-done.5
  436.2 21.8 %while.27 = (s32[]{:T(128)}, bf16[2,768,3,64]{1,3,2,0:T(8,128)(2,1)}, bf16[2,768,3,64]{1,3,2,0:T(8,128)(2,1)}, bf16[2,768,3,64]{1,3,2,0:T(8,128)(2,1)S(1)}, bf16...) while((s32[]{:T(128)}, ...), condition=%wide.region_19.20_spmd, body=%wide.region_17.19_spmd.sunk | while | flops 1160328960 | bytes 67914992 | solution.py:228
  437.8 2.0 fusion.175
  439.7 2.3 multiply_reduce_fusion.16
  442.1 2.0 multiply_convert_fusion.3
  448.6 2.0 fusion.175
  450.6 2.3 multiply_reduce_fusion.16
  452.9 2.0 multiply_convert_fusion.3
  458.1 1.9 copy.187
  462.8 4.2 fusion.117
  467.1 1.6 copy-done.12
  468.7 5.3 fusion.77
  474.0 5.3 fusion.119
  481.7 2.8 fusion.118
  487.4 2.2 multiply_reduce_fusion.1
  489.6 1.8 copy.190
  491.4 1.8 copy.191
  494.9 2.0 pad_maximum_fusion.2
  496.9 64.5 %all-reduce.14.cloned.1.call-done = f32[1536,768]{1,0:T(8,128)} async-done(((f32[1536,768]{1,0:T(8,128)}), f32[1536,768]{1,0:T(8,128)}) %all-reduce.14.cloned.1.call-update) | async-done | bytes 4718608 | tf_op jit(solution)/shard_map/psum | solution.py:239
  561.4 5.7 multiply_reduce_fusion.3
  567.2 39.0 %all-reduce = (f32[2,192]{1,0:T(2,128)S(1)}, f32[768]{0:T(1024)S(1)}, f32[6,768]{1,0:T(8,128)S(1)}, f32[3]{0:T(128)}, f32[]{:T(128)}) all-reduce(f32[2,192]{1,0:T(2,128)S(1)} %pad_maximum_fusion.1, f32[768]{0:T(1024)S(1)} %get-tuple-element.415, f32[6,768]{1,0:T(8,128)S(1)} %stack.39, ...), channel_id=1, replica_groups=mesh['dp'=8,'tensor'=4] {'dp'}, use_global_device_ids=true, to_apply=%region_33.34 | all-reduce | flops 5764 | bytes 46112 | tf_op jit(solution)/shard_map/psum | solution.py:277
  609.3 5.5 fusion.110
  614.8 5.4 add_add_fusion.2
  620.2 181.8 %all-reduce.16.cloned.1.call-done = (f32[768,3,192]{0,2,1:T(8,128)}, f32[192,768]{1,0:T(8,128)}, f32[768,768]{1,0:T(8,128)}, f32[768,768]{0,1:T(8,128)}) async-done(((f32[768,3,192]{0,2,1:T(8,128)}, f32[192,768]{1,0:T(8,128)}, f32[768,768]{1,0:T(8,128)}, f32[768,768]{0,1:T(8,128)}), (f32[768,3,192]{0,2,1:T(8,128)}, f32[192,768]{1,0:T(8,128)}, f32[768,768]{1,0:T(8,128)}, ...) | async-done | bytes 7077904 | tf_op jit(solution)/shard_map/psum | solution.py:277
  802.1 3.0 multiply_reduce_fusion.8
  805.1 2.9 multiply_reduce_fusion.9
  814.9 7.3 psum.109
  824.2 1.9 copy.194
  826.1 1.8 copy.195
  827.9 1.8 copy.196
  829.8 2.2 multiply_subtract_fusion
  832.0 2.2 multiply_subtract_fusion.1
  834.2 1.8 multiply_subtract_fusion.3
  (266 shorter events, 59.3 us)
Async XLA Ops:
  8.0 80.9 %copy-start = (bf16[1,13,768]{2,1,0:T(8,128)(2,1)S(1)}, bf16[1,13,768]{2,1,0:T(8,128)(2,1)}, u32[]{:S(2)}) copy-start(bf16[1,13,768]{2,1,0:T(8,128)(2,1)} %param.32) | copy-start | bytes 59908
  8.1 81.4 %copy-start.56 = (bf16[1,7,768]{2,1,0:T(8,128)(2,1)S(1)}, bf16[1,7,768]{2,1,0:T(8,128)(2,1)}, u32[]{:S(2)}) copy-start(bf16[1,7,768]{2,1,0:T(8,128)(2,1)} %param.33) | copy-start | bytes 32260
  8.1 220.4 %all-reduce.8.cloned.1.call-start = ((), (), s32[]{:S(2)}) async-start(), calls=%async_computation | async-start | bytes 9437184 | tf_op jit(solution)/shard_map/psum | solution.py:158
  12.4 82.7 %copy-start.48 = (f32[768]{0:T(1024)}, f32[768]{0:T(1024)S(1)}, u32[]{:S(2)}) copy-start(f32[768]{0:T(1024)S(1)} %get-tuple-element.344) | copy-start | bytes 9220
  90.0 1.6 copy-start.7
  90.0 2.8 copy-start.3
  93.4 2.9 copy-start.45
  96.3 2.5 copy-start.30
  133.2 103.3 %all-gather.3.cloned.1.call-start = ((), (), s32[]{:S(2)}) async-start(), calls=%async_computation.1 | async-start | bytes 1327104 | tf_op jit(solution)/shard_map/all_gather | solution.py:94
  135.0 108.0 %all-gather.5.cloned.1.call-start = ((), (), s32[]{:S(2)}) async-start(), calls=%async_computation.2 | async-start | bytes 1327104 | tf_op jit(solution)/shard_map/all_gather | solution.py:95
  136.7 182.5 %all-reduce.10.cloned.1.call-start = ((), (), s32[]{:S(2)}) async-start(), calls=%async_computation.3 | async-start | bytes 4718592 | tf_op jit(solution)/shard_map/psum | solution.py:168
  136.7 96.5 %copy-start.57 = (pred[768]{0:T(1024)(128)(4,1)}, pred[768]{0:T(1024)(128)(4,1)S(1)}, u32[]{:S(2)}) copy-start(pred[768]{0:T(1024)(128)(4,1)S(1)} %get-tuple-element.441) | copy-start | bytes 2308
  136.8 96.5 %copy-start.59 = (pred[768]{0:T(1024)(128)(4,1)}, pred[768]{0:T(1024)(128)(4,1)S(1)}, u32[]{:S(2)}) copy-start(pred[768]{0:T(1024)(128)(4,1)S(1)} %get-tuple-element.440) | copy-start | bytes 2308
  233.3 2.2 copy-start.2
  236.5 6.4 copy-start.11
  236.5 6.4 copy-start.53
  242.9 14.5 %copy-start.22 = (f32[1536,768]{1,0:T(8,128)S(1)}, f32[1536,768]{1,0:T(8,128)}, u32[]{:S(2)}) copy-start(f32[1536,768]{1,0:T(8,128)} %fusion.116) | copy-start | bytes 14155780
  257.5 15.5 %copy-start.24 = (bf16[1536,768]{1,0:T(8,128)(2,1)}, bf16[1536,768]{1,0:T(8,128)(2,1)S(1)}, u32[]{:S(2)}) copy-start(bf16[1536,768]{1,0:T(8,128)(2,1)S(1)} %get-tuple-element.416) | copy-start | bytes 7077892
  257.5 2.3 copy-start.62
  263.3 153.0 %all-reduce.12.cloned.1.call-start = ((), (), s32[]{:S(2)}) async-start(), calls=%async_computation.4 | async-start | bytes 9437184 | tf_op jit(solution)/shard_map/psum | solution.py:186
  278.5 137.8 %copy-start.55 = (f32[768]{0:T(1024)S(1)}, f32[768]{0:T(1024)}, u32[]{:S(2)}) copy-start(f32[768]{0:T(1024)} %get-tuple-element.339) | copy-start | bytes 9220
  278.5 149.2 %slice-start = ((s8[4718592]{0:T(1024)(128)(4,1)}), s8[524288]{0:T(1024)(128)(4,1)S(1)}, s32[]{:S(2)}) async-start(s8[4718592]{0:T(1024)(128)(4,1)} %bitcast.196), calls=%async_computation.7 | async-start | bytes 1048576
  278.6 282.8 %all-reduce.14.cloned.1.call-start = ((), (), s32[]{:S(2)}) async-start(), calls=%async_computation.5 | async-start | bytes 9437184 | tf_op jit(solution)/shard_map/psum | solution.py:239
  416.3 11.4 %slice-start.1 = ((s8[4718592]{0:T(1024)(128)(4,1)}), s8[4194304]{0:T(1024)(128)(4,1)S(1)}, s32[]{:S(2)}) async-start(s8[4718592]{0:T(1024)(128)(4,1)} %bitcast.196), calls=%async_computation.8 | async-start | bytes 8388608
  416.3 11.4 %copy-start.10 = (f32[1536,768]{1,0:T(8,128)S(1)}, f32[1536,768]{1,0:T(8,128)}, u32[]{:S(2)}) copy-start(f32[1536,768]{1,0:T(8,128)} %all-reduce.12.cloned.1.call-done) | copy-start | bytes 14155780
  427.7 2.2 copy-start.9
  431.0 2.2 copy-start.5
  433.2 3.0 copy-start.8
  433.2 3.0 copy-start.14
  442.0 2.1 copy-start.26
  442.1 3.3 copy-start.19
  452.9 2.1 copy-start.26
  452.9 3.3 copy-start.19
  458.0 3.5 copy-start.17
  458.0 2.7 copy-start.21
  460.0 2.8 copy-start.38
  467.0 1.7 copy-start.12
  467.0 335.0 %all-reduce.16.cloned.1.call-start = ((), (), s32[]{:S(2)}) async-start(), calls=%async_computation.6 | async-start | bytes 14155776 | tf_op jit(solution)/shard_map/psum | solution.py:277
  468.7 5.3 copy-start.25
  468.7 10.6 %slice-start.2 = ((s8[4718592]{0:T(1024)(128)(4,1)}), s8[4194304]{0:T(1024)(128)(4,1)S(1)}, s32[]{:S(2)}) async-start(s8[4718592]{0:T(1024)(128)(4,1)} %bitcast.198), calls=%async_computation.9 | async-start | bytes 8388608
  474.0 5.3 slice-start.3
  474.0 5.3 copy-start.16
  479.3 1.9 copy-start.31
  479.3 2.4 copy-start.42
  484.6 2.2 copy-start.46
  484.6 8.7 %copy-start.50 = (f32[2,768]{1,0:T(2,128)S(1)}, f32[2,768]{1,0:T(2,128)}, u32[]{:S(2)}) copy-start(f32[2,768]{1,0:T(2,128)} %get-tuple-element.436) | copy-start | bytes 18436
  484.6 8.7 %copy-start.18 = (bf16[2,768,3,64]{1,3,2,0:T(8,128)(2,1)S(1)}, bf16[2,768,3,64]{1,3,2,0:T(8,128)(2,1)}, u32[]{:S(2)}) copy-start(bf16[2,768,3,64]{1,3,2,0:T(8,128)(2,1)} %copy-done.17) | copy-start | bytes 1769476
  484.6 76.8 %copy-start.4 = (bf16[2,768,768]{2,1,0:T(8,128)(2,1)S(1)}, bf16[2,768,768]{2,1,0:T(8,128)(2,1)}, u32[]{:S(2)}) copy-start(bf16[2,768,768]{2,1,0:T(8,128)(2,1)} %param.31) | copy-start | bytes 7077892
  484.6 76.8 %copy-start.49 = (f32[768]{0:T(1024)S(1)}, f32[768]{0:T(1024)}, u32[]{:S(2)}) copy-start(f32[768]{0:T(1024)} %copy-done.48) | copy-start | bytes 9220
  620.2 202.8 %copy-start.35 = (f32[96,3,192]{0,2,1:T(8,128)S(1)}, f32[96,3,192]{0,2,1:T(8,128)}, u32[]{:S(2)}) copy-start(f32[96,3,192]{0,2,1:T(8,128)} %copy.190) | copy-start | bytes 663556
  620.2 202.8 %copy-start.36 = (f32[96,3,192]{0,2,1:T(8,128)S(1)}, f32[96,3,192]{0,2,1:T(8,128)}, u32[]{:S(2)}) copy-start(f32[96,3,192]{0,2,1:T(8,128)} %copy.191) | copy-start | bytes 663556
  802.0 6.0 copy-start.39
  802.0 6.7 copy-start.23
  805.1 24.7 %copy-start.33 = (f32[768,96]{0,1:T(8,128)S(1)}, f32[768,96]{0,1:T(8,128)}, u32[]{:S(2)}) copy-start(f32[768,96]{0,1:T(8,128)} %param.46) | copy-start | bytes 884740
  808.0 24.0 %copy-start.34 = (f32[96,768]{1,0:T(8,128)S(1)}, f32[96,768]{1,0:T(8,128)}, u32[]{:S(2)}) copy-start(f32[96,768]{1,0:T(8,128)} %param.43) | copy-start | bytes 884740
  808.8 25.4 %copy-start.40 = (f32[192,96]{1,0:T(8,128)S(1)}, f32[192,96]{1,0:T(8,128)}, u32[]{:S(2)}) copy-start(f32[192,96]{1,0:T(8,128)} %param.40) | copy-start | bytes 221188
  808.8 25.4 %copy-start.43 = (f32[192,96]{1,0:T(8,128)S(1)}, f32[192,96]{1,0:T(8,128)}, u32[]{:S(2)}) copy-start(f32[192,96]{1,0:T(8,128)} %param.41) | copy-start | bytes 221188
  808.8 30.5 %copy-start.1 = (bf16[1,13,768]{2,1,0:T(8,128)(2,1)S(1)}, bf16[1,13,768]{2,1,0:T(8,128)(2,1)}, u32[]{:S(2)}) copy-start(bf16[1,13,768]{2,1,0:T(8,128)(2,1)} %param.32) | copy-start | bytes 59908
  809.8 26.2 %copy-start.61 = (f32[2,192]{1,0:T(2,128)S(1)}, f32[2,192]{1,0:T(2,128)}, u32[]{:S(2)}) copy-start(f32[2,192]{1,0:T(2,128)} %param.52) | copy-start | bytes 4612
  809.8 27.5 %copy-start.54 = (f32[768]{0:T(1024)S(1)}, f32[768]{0:T(1024)}, u32[]{:S(2)}) copy-start(f32[768]{0:T(1024)} %param.55) | copy-start | bytes 9220
  809.8 28.8 %copy-start.47 = (f32[6,768]{1,0:T(8,128)S(1)}, f32[6,768]{1,0:T(8,128)}, u32[]{:S(2)}) copy-start(f32[6,768]{1,0:T(8,128)} %param.49) | copy-start | bytes 55300
  809.8 28.8 %copy-start.51 = (f32[6,768]{1,0:T(8,128)S(1)}, f32[6,768]{1,0:T(8,128)}, u32[]{:S(2)}) copy-start(f32[6,768]{1,0:T(8,128)} %param.50) | copy-start | bytes 55300
  824.2 10.0 %copy-start.44 = (f32[192,96]{1,0:T(8,128)S(1)}, f32[192,96]{1,0:T(8,128)}, u32[]{:S(2)}) copy-start(f32[192,96]{1,0:T(8,128)} %param.42) | copy-start | bytes 221188
  824.2 14.4 %copy-start.52 = (f32[6,768]{1,0:T(8,128)S(1)}, f32[6,768]{1,0:T(8,128)}, u32[]{:S(2)}) copy-start(f32[6,768]{1,0:T(8,128)} %param.51) | copy-start | bytes 55300
  (17 other events, 18.8 us)
Sparse Core Ops, SparseCore 0:
  133.4 95.1 all-reduce.7
  263.4 55.7 all-reduce.9
  322.2 94.0 all-reduce.11
  467.1 94.1 all-reduce.13
  565.6 236.3 all-reduce.15
Sparse Core Ops, SparseCore 1:
  136.5 42.4 all-gather.2
  181.6 39.9 all-gather.4
where the time goes:
time: 858 us; the launch traced here: 848 us
  waiting for transfers between devices  472 us (55%)
  blocking collectives  119 us (14%)
  other arithmetic  89.4 us (10%)
  matrix products  80.2 us (9%)
  local copies, waits for them, and re-layouts  53.1 us (6%)
  between operations  23.7 us (3%)
  starting transfers between devices  9.92 us (1%)
    psum x1, waiting for transfers between devices, local(): lax.psum((grad_qkv, grad_proj, grad_up, grad_down, vec_part, grad_heads,...  182 us
    psum x1, waiting for transfers between devices, local(): lax.psum(jnp.einsum('rf,df->rd', grad_hidden_low, full_up, preferred_elem...  97.1 us
    psum x1, waiting for transfers between devices, local(): lax.psum(jnp.dot(attended, full_proj, preferred_element_type=jnp.float32)...  88.1 us
    psum x1, waiting for transfers between devices, local(): lax.psum(jnp.einsum('rj,dj->rd', grad_mixed, qkv_matrix, preferred_elemen...  64.5 us
    psum x1, waiting for transfers between devices, local(): lax.psum(jnp.dot(active, full_down, preferred_element_type=jnp.float32).a...  40.6 us
    all_gather x1, blocking collectives, local(): lax.all_gather(w_qkv.astype(jnp.bfloat16), 'dp', axis=0, tiled=True)  39.1 us
    psum x1, blocking collectives, local(): lax.psum((grad_qkv, grad_proj, grad_up, grad_down, vec_part, grad_heads,...  39 us
    all_gather x1, blocking collectives, local(): lax.all_gather(w_proj.astype(jnp.bfloat16), 'dp', axis=1, tiled=True)  33.2 us
  transfers between devices with their start and end apart: 7, of which 5 were waited for; matrix products, arithmetic and copies ran while one was open for 8% of the time, Pallas kernels for 0%

commit v1 on v0

v1 whole, which is shorter than its diff:
```python
import jax
import jax.numpy as jnp
from jax import lax
from jax.sharding import PartitionSpec as P

HD = 64
STEP = 5

norm_eps = 1e-05
clip_limit = 1.0
beta_first = 0.5
beta_second = 0.5
adam_eps = 1e-08
matrix_decay = 0.01
masked_score = -1e30
step_rates = (0.03, 0.2, 0.03, 0.015, 0.3, 0.3, 0.3)
bf16 = jnp.bfloat16
f32 = jnp.float32


def dot(a, b, dims):
    return lax.dot_general(a, b, (dims, ((), ())), preferred_element_type=f32)


NN = ((1,), (0,))
NT = ((1,), (1,))
TN = ((0,), (0,))


def swap_bit(v, axis, size, bit):
    return lax.ppermute(v, axis, [(i, i ^ bit) for i in range(size)])


def norm_parts(stream):
    center = stream - jnp.mean(stream, axis=-1, keepdims=True)
    spread = jnp.mean(center * center, axis=-1, keepdims=True)
    scale = lax.rsqrt(spread + norm_eps)
    return center * scale, scale


def norm_back(scaled, xhat, scale):
    return scale * (
        scaled
        - jnp.mean(scaled, axis=-1, keepdims=True)
        - xhat * jnp.mean(scaled * xhat, axis=-1, keepdims=True)
    )


def segment_ids(lengths_row, rows_count):
    count = lengths_row.shape[0]
    places = jnp.arange(rows_count, dtype=jnp.int32)
    ids = jnp.zeros((rows_count,), jnp.int32)
    bound = jnp.zeros((), jnp.int32)
    for k in range(count):
        bound = bound + lengths_row[k]
        ids = ids + (places >= bound).astype(jnp.int32)
    return ids


def tensor_sum(part, core):
    half = part.shape[0] // 2
    pieces = part.reshape(2, half, part.shape[1])
    away = lax.dynamic_index_in_dim(pieces, 1 - core, 0, False).astype(bf16)
    keep = lax.dynamic_index_in_dim(pieces, core, 0, False).astype(f32)
    low = (keep + swap_bit(away, "tensor", 4, 1).astype(f32)).astype(bf16)
    both = (low.astype(f32) + swap_bit(low, "tensor", 4, 2).astype(f32)).astype(bf16)
    other = swap_bit(both, "tensor", 4, 1)
    return jnp.where(core == 0, jnp.concatenate([both, other]), jnp.concatenate([other, both]))


def scatter_rows(grad, n):
    outer, width = n // 2, grad.shape[1]
    r = grad.shape[0] // n
    me = lax.axis_index("dp")
    inner, mine = me % 2, me // 2
    view = grad.reshape(outer, 2, r, width)
    away = lax.dynamic_index_in_dim(view, 1 - inner, 1, False).astype(bf16)
    keep = lax.dynamic_index_in_dim(view, inner, 1, False).astype(f32)
    half = keep + swap_bit(away, "dp", n, 1).astype(f32)
    low = half.astype(bf16)
    total = lax.dynamic_index_in_dim(half, mine, 0, False)
    for k in range(1, outer):
        block = lax.dynamic_index_in_dim(low, (mine + k) % outer, 0, False)
        pairs = [(i, ((i // 2 + k) % outer) * 2 + i % 2) for i in range(n)]
        total = total + lax.ppermute(block, "dp", pairs).astype(f32)
    return total


def dp_sum(v, n):
    bit = 1
    while bit < n:
        v = v + swap_bit(v, "dp", n, bit)
        bit *= 2
    return v


def adamw_step(weight, moment_old, square_old, gradient, step_rate, decay_value, clip_factor):
    correct_one = 1.0 - beta_first**STEP
    correct_two = 1.0 - beta_second**STEP
    clipped = gradient * clip_factor
    moment_new = beta_first * moment_old + (1.0 - beta_first) * clipped
    square_new = beta_second * square_old + (1.0 - beta_second) * clipped * clipped
    divisor = jnp.sqrt(square_new / correct_two) + adam_eps
    weight_new = weight - step_rate * (moment_new / correct_one / divisor + decay_value * weight)
    return (weight_new, moment_new, square_new)


def attend_forward(queries, keyset, valueset, ids):
    rows = queries.shape[0]
    allowed = ids[:, None] == ids[None, :]
    outs, peaks = [], []
    for h in range(queries.shape[1] // HD):
        cut = slice(h * HD, (h + 1) * HD)
        scores = jnp.where(allowed, dot(queries[:, cut], keyset[:, cut], NT) * HD**-0.5, masked_score)
        peak = jnp.max(scores, axis=-1, keepdims=True)
        exponent = jnp.exp(scores - peak)
        total = jnp.sum(exponent, axis=-1, keepdims=True)
        low = (exponent / total).astype(bf16)
        outs.append(dot(low, valueset[:, cut], NN).astype(bf16))
        peaks.append(peak + jnp.log(total))
    return jnp.concatenate(outs, axis=1), jnp.concatenate(peaks, axis=1)


def attend_backward(queries, keyset, valueset, ids, lse, grad_att):
    allowed = ids[:, None] == ids[None, :]
    dqs, dks, dvs = [], [], []
    for h in range(queries.shape[1] // HD):
        cut = slice(h * HD, (h + 1) * HD)
        q, k, v, g = queries[:, cut], keyset[:, cut], valueset[:, cut], grad_att[:, cut]
        scores = jnp.where(allowed, dot(q, k, NT) * HD**-0.5, masked_score)
        probs = jnp.exp(scores - lse[:, h : h + 1])
        low = probs.astype(bf16)
        grad_probs = dot(g, v, NT)
        inner = jnp.sum(probs * grad_probs, axis=-1, keepdims=True)
        gs = (probs * (grad_probs - inner)).astype(bf16)
        dvs.append(dot(low, g, TN))
        dqs.append(dot(gs, k, NN) * HD**-0.5)
        dks.append(dot(gs, q, TN) * HD**-0.5)
    return jnp.concatenate(dqs + dks + dvs, axis=1).astype(bf16)


def build(n):
    def local(
        inputs,
        time_first,
        time_second,
        lengths_first,
        lengths_second,
        cotangent,
        w_qkv,
        m_qkv,
        v_qkv,
        w_proj,
        m_proj,
        v_proj,
        w_up,
        m_up,
        v_up,
        w_down,
        m_down,
        v_down,
        w_vecs,
        m_vecs,
        v_vecs,
        b_heads,
        m_heads,
        v_heads,
        b_hidden,
        m_hidden,
        v_hidden,
    ):
        rows, features = inputs.shape[1], inputs.shape[2]
        r = w_qkv.shape[0]
        width = w_qkv.shape[2]
        tensor_index = lax.axis_index("tensor")
        core = tensor_index % 2

        first_shard = jnp.concatenate(
            [w_qkv.astype(bf16).reshape(r, 3 * width), w_proj.T.astype(bf16)], axis=1
        )
        bulk_shard = jnp.concatenate([w_up.astype(bf16), w_down.T.astype(bf16)], axis=1)
        bulk = lax.all_gather(bulk_shard, "dp", axis=0, tiled=True)
        first = lax.all_to_all(jnp.tile(first_shard, (n, 1)), "dp", 0, 0, tiled=True)
        qkv_matrix = first[:, : 3 * width]
        proj_own = first[:, 3 * width :]
        hidden_width = w_up.shape[1]
        up_matrix, down_matrix = bulk[:, :hidden_width], bulk[:, hidden_width:]

        def spread(v):
            over_y = swap_bit(v, "tensor", 4, 2)
            return jnp.concatenate(
                [v, swap_bit(v, "tensor", 4, 1), over_y, swap_bit(over_y, "tensor", 4, 1)], axis=1
            )

        proj_all = spread(proj_own)

        halves = []
        for b, (times, lengths) in enumerate(
            ((time_first[0], lengths_first[0]), (time_second[0], lengths_second[0]))
        ):
            seqs = times.shape[0]
            ids = segment_ids(lengths, rows)
            pick = (ids[:, None] == jnp.arange(seqs, dtype=jnp.int32)[None, :]).astype(bf16)
            valid = (ids < seqs).astype(f32)[:, None]
            stream = inputs[b].astype(f32) + dot(pick, times, NN)
            xhat, scale = norm_parts(stream)
            normed = (xhat * w_vecs[0] + w_vecs[1]).astype(bf16)
            upstream = cotangent[b].astype(f32) * valid
            halves.append(
                dict(ids=ids, valid=valid, stream=stream, normed=normed, upstream=upstream)
            )

        for s in halves:
            mixed = dot(s["normed"], qkv_matrix, NN)
            s["q"] = (mixed[:, :width] + b_heads[0]).astype(bf16)
            s["k"] = mixed[:, width : 2 * width].astype(bf16)
            s["v"] = (mixed[:, 2 * width :] + b_heads[1]).astype(bf16)
            s["att"], s["lse"] = attend_forward(s["q"], s["k"], s["v"], s["ids"])
            s["att_all"] = spread(s["att"])

        for s in halves:
            s["branch"] = dot(s["att_all"], proj_all, NT) + w_vecs[4]
            s["middle"] = s["stream"] + s["branch"]
            xhat, scale = norm_parts(s["middle"])
            s["normed_two"] = (xhat * w_vecs[2] + w_vecs[3]).astype(bf16)
            hidden = dot(s["normed_two"], up_matrix, NN) + b_hidden
            cdf = 0.5 * (1.0 + lax.erf(hidden * 0.5**0.5))
            pdf = jnp.exp(-0.5 * hidden * hidden) * 0.3989422804014327
            s["active"] = (hidden * cdf).astype(bf16)
            s["upstream_low"] = s["upstream"].astype(bf16)
            grad_active = dot(s["upstream_low"], down_matrix, NN)
            grad_hidden = grad_active * (cdf + hidden * pdf)
            s["offsets"] = jnp.sum(grad_hidden, axis=0)
            s["grad_hidden"] = grad_hidden.astype(bf16)
            s["gnt"] = tensor_sum(dot(s["grad_hidden"], up_matrix, NT), core)

        for s in halves:
            s["two"] = tensor_sum(dot(s["active"], down_matrix, NT), core)

        def joined(key):
            return jnp.concatenate([s[key] for s in halves])

        grad_up = dot(joined("normed_two"), joined("grad_hidden"), TN)
        grad_down = dot(joined("upstream_low"), joined("active"), TN)
        own_bulk = lax.psum_scatter(
            jnp.concatenate([grad_up, grad_down], axis=1).astype(bf16),
            "dp",
            scatter_dimension=0,
            tiled=True,
        ).astype(f32)

        for s in halves:
            gnt = s["gnt"].astype(f32)
            xhat, scale = norm_parts(s["middle"])
            s["gain_two"] = jnp.sum(gnt * xhat, axis=0)
            s["offset_two"] = jnp.sum(gnt, axis=0)
            grad_middle = s["upstream"] + norm_back(gnt * w_vecs[2], xhat, scale)
            s["grad_middle"] = grad_middle
            s["middle_low"] = grad_middle.astype(bf16)
            grad_att = dot(s["middle_low"], proj_own, NN).astype(bf16)
            s["grad_mixed"] = attend_backward(s["q"], s["k"], s["v"], s["ids"], s["lse"], grad_att)
            s["gn"] = tensor_sum(dot(s["grad_mixed"], qkv_matrix, NT), core)

        grad_first = jnp.concatenate(
            [
                dot(joined("normed"), joined("grad_mixed"), TN),
                dot(joined("middle_low"), joined("att"), TN),
            ],
            axis=1,
        )
        own_first = scatter_rows(grad_first, n)

        block_out, input_grad = [], []
        squares = [0.0, 0.0, 0.0]
        for s in halves:
            two = s["two"].astype(f32) + w_vecs[5]
            total = s["middle"] + two
            block_out.append(total.astype(bf16))
            for i, v in enumerate((total, s["branch"], two)):
                squares[i] = squares[i] + jnp.sum(s["valid"] * v * v)
            gn = s["gn"].astype(f32)
            xhat, scale = norm_parts(s["stream"])
            s["gain_one"] = jnp.sum(gn * xhat, axis=0)
            s["offset_one"] = jnp.sum(gn, axis=0)
            input_grad.append(s["grad_middle"] + norm_back(gn * w_vecs[0], xhat, scale))
        block_out = jnp.stack(block_out)
        input_grad = jnp.stack(input_grad)

        def added(key):
            return halves[0][key] + halves[1][key]

        def summed(key):
            return jnp.sum(halves[0][key], axis=0, dtype=f32) + jnp.sum(
                halves[1][key], axis=0, dtype=f32
            )

        mixed_sums = summed("grad_mixed")
        count = jnp.sum(halves[0]["valid"]) + jnp.sum(halves[1]["valid"])
        scalars = jnp.stack([squares[0], squares[1], squares[2], count])
        message = jnp.stack(
            [
                added("gain_one"),
                added("offset_one"),
                added("gain_two"),
                added("offset_two"),
                summed("grad_middle"),
                summed("upstream"),
                jnp.pad(mixed_sums[:width], (0, features - width)),
                jnp.pad(mixed_sums[2 * width :], (0, features - width)),
                added("offsets"),
                jnp.pad(scalars, (0, features - 4)),
            ]
        )
        message = dp_sum(message, n)
        sum_vecs = message[:6]
        sum_heads = message[6:8, :width]
        sum_hidden = message[8]
        sum_squares, sum_count = message[9, :3], message[9, 3]

        matrix_square = dp_sum(jnp.sum(own_bulk * own_bulk) + jnp.sum(own_first * own_first), n)
        partial_square = matrix_square + jnp.sum(sum_heads * sum_heads) + jnp.sum(
            sum_hidden * sum_hidden
        )
        partial_square = partial_square + swap_bit(partial_square, "tensor", 4, 1)
        partial_square = partial_square + swap_bit(partial_square, "tensor", 4, 2)
        total_square = partial_square + jnp.sum(sum_vecs * sum_vecs)
        grad_norm = jnp.sqrt(total_square)
        clip_factor = jnp.minimum(1.0, clip_limit / (grad_norm + 1e-06))

        updates = (
            (w_qkv, m_qkv, v_qkv, own_first[:, : 3 * width].reshape(r, 3, width), matrix_decay),
            (w_proj, m_proj, v_proj, own_first[:, 3 * width :].T, matrix_decay),
            (w_up, m_up, v_up, own_bulk[:, :hidden_width], matrix_decay),
            (w_down, m_down, v_down, own_bulk[:, hidden_width:].T, matrix_decay),
            (w_vecs, m_vecs, v_vecs, sum_vecs, 0.0),
            (b_heads, m_heads, v_heads, sum_heads, 0.0),
            (b_hidden, m_hidden, v_hidden, sum_hidden, 0.0),
        )
        outs = [block_out, input_grad, grad_norm.reshape(1), jnp.sqrt(sum_squares / (sum_count * features))]
        for (weight, moment, square, gradient, decay), rate in zip(updates, step_rates):
            outs.extend(adamw_step(weight, moment, square, gradient, rate, decay, clip_factor))
        return tuple(outs)

    return local


def solution(mesh):
    rows = P(None, "dp", None)
    group = P("dp", None, None)
    qkv, proj, up = P("dp", None, "tensor"), P("tensor", "dp"), P("dp", "tensor")
    params = [qkv] * 3 + [proj] * 3 + [up] * 3 + [proj] * 3 + [P()] * 3
    params += [P(None, "tensor")] * 3 + [P("tensor")] * 3
    return jax.shard_map(
        build(mesh.shape["dp"]),
        mesh=mesh,
        in_specs=(rows, group, group, P("dp", None), P("dp", None), rows, *params),
        out_specs=(rows, rows, P(), P(), *params),
        check_vma=False,
    )
```

time: 858 us -> 404 us (0.47)
  waiting for transfers between devices: 472 us -> 88.6 us
  blocking collectives: 119 us -> 0 us
  starting transfers between devices: 9.92 us -> 39.5 us
  between operations: 23.7 us -> 42.9 us
  local copies, waits for them, and re-layouts: 53.1 us -> 66.5 us
  matrix products: 80.2 us -> 67.2 us
    psum x5 -> x0, waiting for transfers between devices: 472 us -> none  [the longest x1 182 us: local(): lax.psum((grad_qkv, grad_proj, grad_up, grad_down, vec_part, grad_heads,...]
    ppermute x0 -> x39, waiting for transfers between devices: none -> 76 us  [the longest x36 75.9 us: swap_bit(): return lax.ppermute(v, axis, [(i, i ^ bit) for i in range(size)])]
    all_gather x2 -> x0, blocking collectives: 72.4 us -> none  [the longest x1 39.1 us: local(): lax.all_gather(w_qkv.astype(jnp.bfloat16), 'dp', axis=0, tiled=True)]
    psum x2 -> x0, blocking collectives: 46.4 us -> none  [the longest x1 39 us: local(): lax.psum((grad_qkv, grad_proj, grad_up, grad_down, vec_part, grad_heads,...]
    ppermute x0 -> x39, starting transfers between devices: none -> 32.1 us  [the longest x36 28.3 us: swap_bit(): return lax.ppermute(v, axis, [(i, i ^ bit) for i in range(size)])]
    unnamed x133 -> x383, local copies, waits for them, and re-layouts: 24.9 us -> 42.8 us
    while x36 -> x0, local copies, waits for them, and re-layouts: 13.3 us -> none  [the longest x4 6.7 us: local(): lax.map(attend_forward, (query_halves, key_halves, value_halves, segment_...]
    dot_general x28 -> x58, matrix products: 80.2 us -> 67.2 us  [dot(): return lax.dot_general(a, b, (dims, ((), ())), preferred_element_type=f32)]
  transfers between devices with their start and end apart: 7 -> 42, of which waited for: 5 -> 16; matrix products, arithmetic and copies ran while one was open for 8% -> 45% of each run, Pallas kernels for 0% -> 0%
where the time goes in v1:
time: 404 us; the launch traced here: 398 us
  other arithmetic  93.8 us (23%)
  waiting for transfers between devices  88.6 us (22%)
  matrix products  67.2 us (17%)
  local copies, waits for them, and re-layouts  66.5 us (16%)
  between operations  42.9 us (11%)
  starting transfers between devices  39.5 us (10%)
    ppermute x36, waiting for transfers between devices, swap_bit(): return lax.ppermute(v, axis, [(i, i ^ bit) for i in range(size)])  75.9 us
    dot_general x58, matrix products, dot(): return lax.dot_general(a, b, (dims, ((), ())), preferred_element_type=f32)  67.2 us
    unnamed x383, local copies, waits for them, and re-layouts  42.8 us
    ppermute x36, starting transfers between devices, swap_bit(): return lax.ppermute(v, axis, [(i, i ^ bit) for i in range(size)])  28.3 us
    all_to_all x1, waiting for transfers between devices, local(): lax.all_to_all(jnp.tile(first_shard, (n, 1)), 'dp', 0, 0, tiled=True)  12.6 us
    reduce_sum x2, other arithmetic, local(): s['gain_two'] = jnp.sum(gnt * xhat, axis=0)  11 us
  transfers between devices with their start and end apart: 42, of which 16 were waited for; matrix products, arithmetic and copies ran while one was open for 45% of the time, Pallas kernels for 0%

profile of v1, /device:TPU:0, one launch (start us, length us, event | category | flops | bytes accessed | tf_op | source)
XLA Modules:
  0.0 398.5 jit_solution(16810276348175593337)
XLA Ops:
  10.6 7.4 %all-to-all-start = ((bf16[8,96,768]{2,1,0:T(8,128)(2,1)}), bf16[8,96,768]{2,1,0:T(8,128)(2,1)S(1)}, u32[]{:S(2)}, u32[]{:S(2)}) async-start(bf16[8,96,768]{2,1,0:T(8,128)(2,1)} %tile.2), calls=%async_computation | async-start | bytes 2359296 | tf_op jit(solution)/shard_map/all_to_all | solution.py:183
  35.1 2.0 fusion.351
  40.9 2.5 add_convert_fusion.3
  43.5 12.6 %all-to-all-done = bf16[8,96,768]{2,1,0:T(8,128)(2,1)S(1)} async-done(((bf16[8,96,768]{2,1,0:T(8,128)(2,1)}), bf16[8,96,768]{2,1,0:T(8,128)(2,1)S(1)}, u32[]{:S(2)}, u32[]{:S(2)}) %all-to-all-start) | async-done | bytes 1179680 | tf_op jit(solution)/shard_map/all_to_all | solution.py:183
  56.1 2.3 fusion.353
  67.8 1.6 collective-permute-start.1
  78.9 1.6 collective-permute-start.4
  81.1 1.7 constant_dynamic-update-slice_fusion.2
  82.8 1.7 constant_dynamic-update-slice_fusion.1
  84.5 3.2 collective-permute-done.10
  87.7 7.7 %collective-permute-done.4 = bf16[768,192]{1,0:T(8,128)(2,1)} collective-permute-done((bf16[768,192]{1,0:T(8,128)(2,1)}, bf16[768,192]{1,0:T(8,128)(2,1)}, u32[]{:S(2)}, u32[]{:S(2)}) %collective-permute-start.4) | collective-permute-done | bytes 294944 | tf_op jit(solution)/shard_map/ppermute | solution.py:31
  95.5 1.7 constant_dynamic-update-slice_fusion.8
  97.2 1.7 constant_dynamic-update-slice_fusion.7
  100.4 3.3 fusion.314
  103.7 5.1 %fusion.343 = (f32[768]{0:T(1024)S(1)}, f32[768,768]{1,0:T(8,128)S(1)}, f32[768]{0:T(1024)S(1)}, f32[768,768]{1,0:T(8,128)S(1)}, f32[768,768]{1,0:T(8,128)}) fusion(f32[768,768]{1,0:T(8,128)S(1)} %copy-done.3, f32[768]{0:T(1024)S(1)} %copy-done.121, f32[768,768]{1,0:T(8,128)S(1)} %get-tuple-element.274, f32[768,768]{1,0:T(8,128)S(1)} %fusion.314, ...), kind=kOutput, calls=%fused_computation.540 | convolution fusion | flops 914225664 | bytes 16524288 | tf_op jit(solution)/shard_map/dot_general | solution.py:22
  111.1 2.0 add_convert_fusion.2
  113.0 2.9 fusion.213
  115.9 3.2 multiply_convert_fusion.7
  127.0 1.6 copy.171
  128.6 1.8 copy.167
  130.5 1.6 copy.168
  132.1 1.6 copy.169
  133.7 1.8 copy.163
  135.5 1.8 copy.165
  141.2 1.7 fusion.123
  143.4 1.7 fusion.124
  145.2 1.7 collective-permute-start.7
  148.2 11.1 %collective-permute-done.13 = bf16[384,768]{1,0:T(8,128)(2,1)S(1)} collective-permute-done((bf16[384,768]{1,0:T(8,128)(2,1)S(1)}, bf16[384,768]{1,0:T(8,128)(2,1)S(1)}, u32[]{:S(2)}, u32[]{:S(2)}) %collective-permute-start.13) | collective-permute-done | bytes 589856 | tf_op jit(solution)/shard_map/ppermute | solution.py:31
  159.4 11.5 %collective-permute-done.7 = bf16[384,768]{1,0:T(8,128)(2,1)S(1)} collective-permute-done((bf16[384,768]{1,0:T(8,128)(2,1)S(1)}, bf16[384,768]{1,0:T(8,128)(2,1)S(1)}, u32[]{:S(2)}, u32[]{:S(2)}) %collective-permute-start.7) | collective-permute-done | bytes 589856 | tf_op jit(solution)/shard_map/ppermute | solution.py:31
  173.2 5.0 %fusion.72 = (f32[768]{0:T(1024)S(1)}, f32[768]{0:T(1024)S(1)}, f32[]{:T(128)}, f32[]{:T(128)}, f32[]{:T(128)}, /*index=5*/f32[]{:T(128)}, bf16[768,768]{1,0:T(8,128)(2,1)S(1)}, bf16[768,768]{1,0:T(8,128)(2,1)S(1)}) fusion(f32[768]{0:T(1024)S(1)} %copy-done.115, bf16[2,768,768]{2,1,0:T(8,128)(2,1)S(1)} %copy-done.30, f32[768]{0:T(1024)S(1)} %copy-done.117, ...), kind=kLoop, calls=%fused_computation.103 | loop fusion | flops 25950716 | bytes 11814929 | tf_op jit(solution)/shard_map/reduce_sum | solution.py:293
  178.2 2.2 fusion.346
  182.1 2.4 fusion.345
  187.2 2.1 fusion.98
  191.4 11.1 %collective-permute-done.16 = bf16[384,768]{1,0:T(8,128)(2,1)S(1)} collective-permute-done((bf16[384,768]{1,0:T(8,128)(2,1)S(1)}, bf16[384,768]{1,0:T(8,128)(2,1)S(1)}, u32[]{:S(2)}, u32[]{:S(2)}) %collective-permute-start.16) | collective-permute-done | bytes 589856 | tf_op jit(solution)/shard_map/ppermute | solution.py:31
  203.4 2.0 fusion.93
  208.3 4.3 %copy.178 = bf16[768,1536]{1,0:T(8,128)(2,1)} copy(bf16[768,1536]{0,1:T(8,128)(2,1)} %pad_maximum_fusion.2) | data formatting | bytes 4718592
  217.2 5.8 %fusion.35 = (f32[768]{0:T(1024)}, f32[768]{0:T(1024)S(1)}, f32[]{:T(128)}, bf16[1,768,768]{2,1,0:T(8,128)(2,1)}) fusion(f32[768,768]{1,0:T(8,128)} %copy-done.7, f32[768]{0:T(1024)} %copy-done.113, f32[768]{0:T(1024)} %copy-done.84, bf16[384,768]{1,0:T(8,128)(2,1)} %add_convert_fusion.7, bf16[384,768]{1,0:T(8,128)(2,1)} %collective-permute-done.17, ...), kind=kLoop, calls=%fused_computation.62 | loop fusion | flops 19462656 | bytes 5919749 | tf_op jit(solution)/shard_map/reduce_sum | solution.py:255
  223.0 2.7 convert_reduce_fusion.3
  225.8 5.6 %fusion.339 = (f32[768]{0:T(1024)}, f32[768,768]{1,0:T(8,128)S(1)}, f32[768]{0:T(1024)S(1)}, f32[768]{0:T(1024)}) fusion(f32[768]{0:T(1024)S(1)} %broadcast_multiply_fusion.6, f32[768,768]{1,0:T(8,128)S(1)} %copy-done.8, f32[768]{0:T(1024)S(1)} %copy-done.85, f32[768]{0:T(1024)S(1)} %broadcast_multiply_fusion.7, f32[768]{0:T(1024)S(1)} %get-tuple-element.168, ...), kind=kLoop, calls=%fused_computation.538 | loop fusion | flops 20051712 | bytes 8285185 | tf_op jit(solution)/shard_map/reduce_sum | solution.py:293
  247.1 5.1 %fusion.42 = (f32[768]{0:T(1024)}, f32[768]{0:T(1024)S(1)}, f32[]{:T(128)}, bf16[1,768,768]{2,1,0:T(8,128)(2,1)}) fusion(f32[768,768]{1,0:T(8,128)S(1)} %copy-done.6, f32[768]{0:T(1024)S(1)} %copy-done.112, f32[768]{0:T(1024)S(1)} %copy-done.83, bf16[384,768]{1,0:T(8,128)(2,1)S(1)} %add_convert_fusion.5, bf16[384,768]{1,0:T(8,128)(2,1)S(1)} %collective-permute-done.23, ...), kind=kLoop, calls=%fused_computation.69 | loop fusion | flops 19462656 | bytes 5919749 | tf_op jit(solution)/shard_map/reduce_sum | solution.py:255
  252.2 2.7 fusion.337
  279.6 3.3 copy.162
  287.8 1.7 collective-permute-start.25
  291.9 11.6 %collective-permute-done.19 = bf16[384,768]{1,0:T(8,128)(2,1)S(1)} collective-permute-done((bf16[384,768]{1,0:T(8,128)(2,1)S(1)}, bf16[384,768]{1,0:T(8,128)(2,1)S(1)}, u32[]{:S(2)}, u32[]{:S(2)}) %collective-permute-start.19) | collective-permute-done | bytes 589856 | tf_op jit(solution)/shard_map/ppermute | solution.py:31
  303.7 11.4 %collective-permute-done.25 = bf16[384,768]{1,0:T(8,128)(2,1)S(1)} collective-permute-done((bf16[384,768]{1,0:T(8,128)(2,1)S(1)}, bf16[384,768]{1,0:T(8,128)(2,1)S(1)}, u32[]{:S(2)}, u32[]{:S(2)}) %collective-permute-start.25) | collective-permute-done | bytes 589856 | tf_op jit(solution)/shard_map/ppermute | solution.py:31
  320.3 1.8 collective-permute-start.29
  322.1 2.0 collective-permute-start.30
  324.2 3.9 fusion.36
  328.2 2.9 convert_reduce_fusion.2
  331.0 2.9 convert_reduce_fusion
  334.0 2.7 stack.66
  337.9 3.0 pad_maximum_fusion.1
  342.4 1.9 multiply_reduce_fusion.11
  344.3 1.6 collective-permute-done.35
  345.9 2.1 collective-permute-start.36
  348.0 2.5 pad_maximum_fusion
  355.1 1.7 multiply_reduce_fusion.10
  358.1 2.6 collective-permute-start.31
  363.9 2.0 collective-permute-done.32
  366.6 2.9 collective-permute-start.33
  369.5 1.6 collective-permute-done.33
  374.7 1.9 collective-permute-start.38
  376.7 1.6 collective-permute-done.38
  386.5 2.0 multiply_subtract_fusion
  (608 shorter events, 130.6 us)
Async XLA Ops:
  7.2 27.8 %copy-start = (bf16[1,13,768]{2,1,0:T(8,128)(2,1)S(1)}, bf16[1,13,768]{2,1,0:T(8,128)(2,1)}, u32[]{:S(2)}) copy-start(bf16[1,13,768]{2,1,0:T(8,128)(2,1)} %param.28) | copy-start | bytes 59908
  10.6 45.5 %all-to-all-start = ((bf16[8,96,768]{2,1,0:T(8,128)(2,1)}), bf16[8,96,768]{2,1,0:T(8,128)(2,1)S(1)}, u32[]{:S(2)}, u32[]{:S(2)}) async-start(bf16[8,96,768]{2,1,0:T(8,128)(2,1)} %tile.2), calls=%async_computation | async-start | bytes 2359296 | tf_op jit(solution)/shard_map/all_to_all | solution.py:183
  18.0 95.0 %all-gather.2.cloned.1.call-start = ((), (), s32[]{:S(2)}) async-start(), calls=%async_computation.2 | async-start | bytes 2654208 | tf_op jit(solution)/shard_map/all_gather | solution.py:182
  18.9 336.2 %reduce-scatter.4.cloned.1.call-start = ((), (), s32[]{:S(2)}) async-start(), calls=%async_computation.3 | async-start | bytes 2654208 | tf_op jit(solution)/shard_map/reduce_scatter | solution.py:245
  67.8 12.7 %collective-permute-start = (bf16[768,192]{0,1:T(8,128)(2,1)}, bf16[768,192]{0,1:T(8,128)(2,1)}, u32[]{:S(2)}, u32[]{:S(2)}) collective-permute-start(bf16[768,192]{0,1:T(8,128)(2,1)} %pad_maximum_fusion.5), channel_id=1, source_target_pairs={{0,1},{1,0},{2,3},{3,2},{4,5},{5,4},{6,7},{7,6},{8,9},{9,8},{10,11... | collective-permute-start | bytes 884744 | tf_op jit(solution)/shard_map/ppermute | solution.py:31
  67.8 13.2 %collective-permute-start.1 = (bf16[768,192]{0,1:T(8,128)(2,1)}, bf16[768,192]{0,1:T(8,128)(2,1)}, u32[]{:S(2)}, u32[]{:S(2)}) collective-permute-start(bf16[768,192]{0,1:T(8,128)(2,1)} %pad_maximum_fusion.5), channel_id=1, source_target_pairs={{0,2},{1,3},{2,0},{3,1},{4,6},{5,7},{6,4},{7,5},{8,10},{9,11},{10,... | collective-permute-start | bytes 884744 | tf_op jit(solution)/shard_map/ppermute | solution.py:31
  77.6 10.2 %collective-permute-start.10 = (bf16[768,192]{0,1:T(8,128)(2,1)}, bf16[768,192]{0,1:T(8,128)(2,1)}, u32[]{:S(2)}, u32[]{:S(2)}) collective-permute-start(bf16[768,192]{0,1:T(8,128)(2,1)} %pad_maximum_fusion.7), channel_id=1, source_target_pairs={{0,2},{1,3},{2,0},{3,1},{4,6},{5,7},{6,4},{7,5},{8,10},{9,11},{10,... | collective-permute-start | bytes 884744 | tf_op jit(solution)/shard_map/ppermute | solution.py:31
  78.9 16.6 %collective-permute-start.4 = (bf16[768,192]{1,0:T(8,128)(2,1)}, bf16[768,192]{1,0:T(8,128)(2,1)}, u32[]{:S(2)}, u32[]{:S(2)}) collective-permute-start(bf16[768,192]{1,0:T(8,128)(2,1)} %slice.372), channel_id=1, source_target_pairs={{0,2},{1,3},{2,0},{3,1},{4,6},{5,7},{6,4},{7,5},{8,10},{9,11},{10,... | collective-permute-start | bytes 884744 | tf_op jit(solution)/shard_map/ppermute | solution.py:31
  80.5 14.9 %collective-permute-start.9 = (bf16[768,192]{0,1:T(8,128)(2,1)}, bf16[768,192]{0,1:T(8,128)(2,1)}, u32[]{:S(2)}, u32[]{:S(2)}) collective-permute-start(bf16[768,192]{0,1:T(8,128)(2,1)} %pad_maximum_fusion.7), channel_id=1, source_target_pairs={{0,1},{1,0},{2,3},{3,2},{4,5},{5,4},{6,7},{7,6},{8,9},{9,8},{10,11... | collective-permute-start | bytes 884744 | tf_op jit(solution)/shard_map/ppermute | solution.py:31
  80.5 19.8 %collective-permute-start.3 = (bf16[768,192]{1,0:T(8,128)(2,1)}, bf16[768,192]{1,0:T(8,128)(2,1)S(1)}, u32[]{:S(2)}, u32[]{:S(2)}) collective-permute-start(bf16[768,192]{1,0:T(8,128)(2,1)} %slice.372), channel_id=1, source_target_pairs={{0,1},{1,0},{2,3},{3,2},{4,5},{5,4},{6,7},{7,6},{8,9},{9,8},{10,11... | collective-permute-start | bytes 884744 | tf_op jit(solution)/shard_map/ppermute | solution.py:31
  81.0 17.8 %collective-permute-start.2 = (bf16[768,192]{0,1:T(8,128)(2,1)}, bf16[768,192]{0,1:T(8,128)(2,1)S(1)}, u32[]{:S(2)}, u32[]{:S(2)}) collective-permute-start(bf16[768,192]{0,1:T(8,128)(2,1)} %collective-permute-done.1), channel_id=1, source_target_pairs={{0,1},{1,0},{2,3},{3,2},{4,5},{5,4},{6,7},{7,6},{8,9},{9,8},{10,11... | collective-permute-start | bytes 884744 | tf_op jit(solution)/shard_map/ppermute | solution.py:31
  87.7 11.9 %collective-permute-start.11 = (bf16[768,192]{0,1:T(8,128)(2,1)}, bf16[768,192]{0,1:T(8,128)(2,1)S(1)}, u32[]{:S(2)}, u32[]{:S(2)}) collective-permute-start(bf16[768,192]{0,1:T(8,128)(2,1)} %collective-permute-done.10), channel_id=1, source_target_pairs={{0,1},{1,0},{2,3},{3,2},{4,5},{5,4},{6,7},{7,6},{8,9},{9,8},{10,11... | collective-permute-start | bytes 884744 | tf_op jit(solution)/shard_map/ppermute | solution.py:31
  95.5 4.9 %collective-permute-start.5 = (bf16[768,192]{1,0:T(8,128)(2,1)}, bf16[768,192]{1,0:T(8,128)(2,1)S(1)}, u32[]{:S(2)}, u32[]{:S(2)}) collective-permute-start(bf16[768,192]{1,0:T(8,128)(2,1)} %collective-permute-done.4), channel_id=1, source_target_pairs={{0,1},{1,0},{2,3},{3,2},{4,5},{5,4},{6,7},{7,6},{8,9},{9,8},{10,11... | collective-permute-start | bytes 884744 | tf_op jit(solution)/shard_map/ppermute | solution.py:31
  121.2 20.0 %collective-permute-start.12 = (bf16[384,768]{1,0:T(8,128)(2,1)}, bf16[384,768]{1,0:T(8,128)(2,1)}, u32[]{:S(2)}, u32[]{:S(2)}) collective-permute-start(bf16[384,768]{1,0:T(8,128)(2,1)} %fusion.226), channel_id=1, source_target_pairs={{0,1},{1,0},{2,3},{3,2},{4,5},{5,4},{6,7},{7,6},{8,9},{9,8},{10,11... | collective-permute-start | bytes 1769480 | tf_op jit(solution)/shard_map/ppermute | solution.py:31
  125.2 18.1 %collective-permute-start.6 = (bf16[384,768]{1,0:T(8,128)(2,1)}, bf16[384,768]{1,0:T(8,128)(2,1)}, u32[]{:S(2)}, u32[]{:S(2)}) collective-permute-start(bf16[384,768]{1,0:T(8,128)(2,1)} %fusion.225), channel_id=1, source_target_pairs={{0,1},{1,0},{2,3},{3,2},{4,5},{5,4},{6,7},{7,6},{8,9},{9,8},{10,11... | collective-permute-start | bytes 1769480 | tf_op jit(solution)/shard_map/ppermute | solution.py:31
  141.2 31.9 %copy-start.30 = (bf16[2,768,768]{2,1,0:T(8,128)(2,1)S(1)}, bf16[2,768,768]{2,1,0:T(8,128)(2,1)}, u32[]{:S(2)}) copy-start(bf16[2,768,768]{2,1,0:T(8,128)(2,1)} %param.32) | copy-start | bytes 7077892
  143.0 16.3 %collective-permute-start.13 = (bf16[384,768]{1,0:T(8,128)(2,1)S(1)}, bf16[384,768]{1,0:T(8,128)(2,1)S(1)}, u32[]{:S(2)}, u32[]{:S(2)}) collective-permute-start(bf16[384,768]{1,0:T(8,128)(2,1)S(1)} %fusion.123), channel_id=1, source_target_pairs={{0,2},{1,3},{2,0},{3,1},{4,6},{5,7},{6,4},{7,5},{8,10},{9,11},{10,... | collective-permute-start | bytes 1769480 | tf_op jit(solution)/shard_map/ppermute | solution.py:31
  143.4 29.7 %copy-start.27 = (f32[768,768]{1,0:T(8,128)S(1)}, f32[768,768]{1,0:T(8,128)}, u32[]{:S(2)}) copy-start(f32[768,768]{1,0:T(8,128)} %get-tuple-element.303) | copy-start | bytes 7077892
  145.1 26.7 %copy-start.140 = (f32[768]{0:T(1024)S(1)}, f32[768]{0:T(1024)}, u32[]{:S(2)}) copy-start(f32[768]{0:T(1024)} %copy-done.139) | copy-start | bytes 9220
  145.1 26.7 %copy-start.146 = (f32[768]{0:T(1024)S(1)}, f32[768]{0:T(1024)}, u32[]{:S(2)}) copy-start(f32[768]{0:T(1024)} %copy-done.145) | copy-start | bytes 9220
  145.2 27.3 %copy-start.142 = (f32[768]{0:T(1024)S(1)}, f32[768]{0:T(1024)}, u32[]{:S(2)}) copy-start(f32[768]{0:T(1024)} %copy-done.141) | copy-start | bytes 9220
  145.2 27.3 %copy-start.144 = (f32[768]{0:T(1024)S(1)}, f32[768]{0:T(1024)}, u32[]{:S(2)}) copy-start(f32[768]{0:T(1024)} %copy-done.143) | copy-start | bytes 9220
  145.2 28.0 %copy-start.26 = (f32[768,768]{1,0:T(8,128)S(1)}, f32[768,768]{1,0:T(8,128)}, u32[]{:S(2)}) copy-start(f32[768,768]{1,0:T(8,128)} %copy-done.25) | copy-start | bytes 7077892
  145.2 27.9 %copy-start.115 = (f32[768]{0:T(1024)S(1)}, f32[768]{0:T(1024)}, u32[]{:S(2)}) copy-start(f32[768]{0:T(1024)} %get-tuple-element.321) | copy-start | bytes 9220
  145.2 27.9 %copy-start.117 = (f32[768]{0:T(1024)S(1)}, f32[768]{0:T(1024)}, u32[]{:S(2)}) copy-start(f32[768]{0:T(1024)} %get-tuple-element.322) | copy-start | bytes 9220
  145.2 27.9 %copy-start.119 = (f32[768]{0:T(1024)S(1)}, f32[768]{0:T(1024)}, u32[]{:S(2)}) copy-start(f32[768]{0:T(1024)} %get-tuple-element.173) | copy-start | bytes 9220
  145.2 27.9 %copy-start.122 = (f32[768]{0:T(1024)S(1)}, f32[768]{0:T(1024)}, u32[]{:S(2)}) copy-start(f32[768]{0:T(1024)} %get-tuple-element.170) | copy-start | bytes 9220
  145.2 25.7 %collective-permute-start.7 = (bf16[384,768]{1,0:T(8,128)(2,1)S(1)}, bf16[384,768]{1,0:T(8,128)(2,1)S(1)}, u32[]{:S(2)}, u32[]{:S(2)}) collective-permute-start(bf16[384,768]{1,0:T(8,128)(2,1)S(1)} %fusion.124), channel_id=1, source_target_pairs={{0,2},{1,3},{2,0},{3,1},{4,6},{5,7},{6,4},{7,5},{8,10},{9,11},{10,... | collective-permute-start | bytes 1769480 | tf_op jit(solution)/shard_map/ppermute | solution.py:31
  159.4 13.7 %collective-permute-start.14 = (bf16[384,768]{1,0:T(8,128)(2,1)S(1)}, bf16[384,768]{1,0:T(8,128)(2,1)S(1)}, u32[]{:S(2)}, u32[]{:S(2)}) collective-permute-start(bf16[384,768]{1,0:T(8,128)(2,1)S(1)} %add_convert_fusion.8), channel_id=1, source_target_pairs={{0,1},{1,0},{2,3},{3,2},{4,5},{5,4},{6,7},{7,6},{8,9},{9,8},{10,11... | collective-permute-start | bytes 1769480 | tf_op jit(solution)/shard_map/ppermute | solution.py:31
  171.0 2.1 collective-permute-start.8
  181.6 4.5 %collective-permute-start.15 = (bf16[384,768]{1,0:T(8,128)(2,1)S(1)}, bf16[384,768]{1,0:T(8,128)(2,1)S(1)}, u32[]{:S(2)}, u32[]{:S(2)}) collective-permute-start(bf16[384,768]{1,0:T(8,128)(2,1)S(1)} %fusion.227), channel_id=1, source_target_pairs={{0,1},{1,0},{2,3},{3,2},{4,5},{5,4},{6,7},{7,6},{8,9},{9,8},{10,11... | collective-permute-start | bytes 1769480 | tf_op jit(solution)/shard_map/ppermute | solution.py:31
  185.7 3.6 collective-permute-start.21
  186.2 16.2 %collective-permute-start.16 = (bf16[384,768]{1,0:T(8,128)(2,1)S(1)}, bf16[384,768]{1,0:T(8,128)(2,1)S(1)}, u32[]{:S(2)}, u32[]{:S(2)}) collective-permute-start(bf16[384,768]{1,0:T(8,128)(2,1)S(1)} %fusion.122), channel_id=1, source_target_pairs={{0,2},{1,3},{2,0},{3,1},{4,6},{5,7},{6,4},{7,5},{8,10},{9,11},{10,... | collective-permute-start | bytes 1769480 | tf_op jit(solution)/shard_map/ppermute | solution.py:31
  190.2 24.9 %collective-permute-start.22 = (bf16[384,768]{1,0:T(8,128)(2,1)}, bf16[384,768]{1,0:T(8,128)(2,1)}, u32[]{:S(2)}, u32[]{:S(2)}) collective-permute-start(bf16[384,768]{1,0:T(8,128)(2,1)} %fusion.120), channel_id=1, source_target_pairs={{0,2},{1,3},{2,0},{3,1},{4,6},{5,7},{6,4},{7,5},{8,10},{9,11},{10,... | collective-permute-start | bytes 1769480 | tf_op jit(solution)/shard_map/ppermute | solution.py:31
  203.4 13.7 %collective-permute-start.17 = (bf16[384,768]{1,0:T(8,128)(2,1)}, bf16[384,768]{1,0:T(8,128)(2,1)}, u32[]{:S(2)}, u32[]{:S(2)}) collective-permute-start(bf16[384,768]{1,0:T(8,128)(2,1)} %add_convert_fusion.7), channel_id=1, source_target_pairs={{0,1},{1,0},{2,3},{3,2},{4,5},{5,4},{6,7},{7,6},{8,9},{9,8},{10,11... | collective-permute-start | bytes 1769480 | tf_op jit(solution)/shard_map/ppermute | solution.py:31
  216.6 9.2 %collective-permute-start.23 = (bf16[384,768]{1,0:T(8,128)(2,1)S(1)}, bf16[384,768]{1,0:T(8,128)(2,1)S(1)}, u32[]{:S(2)}, u32[]{:S(2)}) collective-permute-start(bf16[384,768]{1,0:T(8,128)(2,1)S(1)} %add_convert_fusion.5), channel_id=1, source_target_pairs={{0,1},{1,0},{2,3},{3,2},{4,5},{5,4},{6,7},{7,6},{8,9},{9,8},{10,11... | collective-permute-start | bytes 1769480 | tf_op jit(solution)/shard_map/ppermute | solution.py:31
  275.9 9.8 %collective-permute-start.18 = (bf16[384,768]{1,0:T(8,128)(2,1)}, bf16[384,768]{1,0:T(8,128)(2,1)S(1)}, u32[]{:S(2)}, u32[]{:S(2)}) collective-permute-start(bf16[384,768]{1,0:T(8,128)(2,1)} %fusion.228), channel_id=1, source_target_pairs={{0,1},{1,0},{2,3},{3,2},{4,5},{5,4},{6,7},{7,6},{8,9},{9,8},{10,11... | collective-permute-start | bytes 1769480 | tf_op jit(solution)/shard_map/ppermute | solution.py:31
  276.8 10.9 %collective-permute-start.24 = (bf16[384,768]{1,0:T(8,128)(2,1)}, bf16[384,768]{1,0:T(8,128)(2,1)S(1)}, u32[]{:S(2)}, u32[]{:S(2)}) collective-permute-start(bf16[384,768]{1,0:T(8,128)(2,1)} %fusion.230), channel_id=1, source_target_pairs={{0,1},{1,0},{2,3},{3,2},{4,5},{5,4},{6,7},{7,6},{8,9},{9,8},{10,11... | collective-permute-start | bytes 1769480 | tf_op jit(solution)/shard_map/ppermute | solution.py:31
  287.2 16.3 %collective-permute-start.19 = (bf16[384,768]{1,0:T(8,128)(2,1)S(1)}, bf16[384,768]{1,0:T(8,128)(2,1)S(1)}, u32[]{:S(2)}, u32[]{:S(2)}) collective-permute-start(bf16[384,768]{1,0:T(8,128)(2,1)S(1)} %fusion.121), channel_id=1, source_target_pairs={{0,2},{1,3},{2,0},{3,1},{4,6},{5,7},{6,4},{7,5},{8,10},{9,11},{10,... | collective-permute-start | bytes 1769480 | tf_op jit(solution)/shard_map/ppermute | solution.py:31
  287.8 27.3 %collective-permute-start.25 = (bf16[384,768]{1,0:T(8,128)(2,1)S(1)}, bf16[384,768]{1,0:T(8,128)(2,1)S(1)}, u32[]{:S(2)}, u32[]{:S(2)}) collective-permute-start(bf16[384,768]{1,0:T(8,128)(2,1)S(1)} %fusion.119), channel_id=1, source_target_pairs={{0,2},{1,3},{2,0},{3,1},{4,6},{5,7},{6,4},{7,5},{8,10},{9,11},{10,... | collective-permute-start | bytes 1769480 | tf_op jit(solution)/shard_map/ppermute | solution.py:31
  290.2 28.2 %collective-permute-start.27 = (bf16[4,96,768]{2,1,0:T(8,128)(2,1)S(1)}, bf16[4,96,768]{2,1,0:T(8,128)(2,1)S(1)}, u32[]{:S(2)}, u32[]{:S(2)}) collective-permute-start(bf16[4,96,768]{2,1,0:T(8,128)(2,1)S(1)} %fusion.231), channel_id=1, source_target_pairs={{0,4},{4,0},{8,12},{12,8},{16,20},{20,16},{24,28},{28,24},{1,5},{5... | collective-permute-start | bytes 1769480 | tf_op jit(solution)/shard_map/ppermute | solution.py:31
  291.6 26.1 %copy-start.157 = (f32[768]{0:T(1024)S(1)}, f32[768]{0:T(1024)}, u32[]{:S(2)}) copy-start(f32[768]{0:T(1024)} %get-tuple-element.152) | copy-start | bytes 9220
  291.6 26.1 %copy-start.158 = (f32[768]{0:T(1024)S(1)}, f32[768]{0:T(1024)}, u32[]{:S(2)}) copy-start(f32[768]{0:T(1024)} %get-tuple-element.150) | copy-start | bytes 9220
  291.7 26.7 %copy-start.32 = (f32[768,768]{1,0:T(8,128)S(1)}, f32[768,768]{1,0:T(8,128)}, u32[]{:S(2)}) copy-start(f32[768,768]{1,0:T(8,128)} %copy.162) | copy-start | bytes 7077892
  303.6 20.5 %collective-permute-start.20 = (bf16[384,768]{1,0:T(8,128)(2,1)S(1)}, bf16[384,768]{1,0:T(8,128)(2,1)S(1)}, u32[]{:S(2)}, u32[]{:S(2)}) collective-permute-start(bf16[384,768]{1,0:T(8,128)(2,1)S(1)} %add_convert_fusion.6), channel_id=1, source_target_pairs={{0,1},{1,0},{2,3},{3,2},{4,5},{5,4},{6,7},{7,6},{8,9},{9,8},{10,11... | collective-permute-start | bytes 1769480 | tf_op jit(solution)/shard_map/ppermute | solution.py:31
  315.3 8.8 %collective-permute-start.26 = (bf16[384,768]{1,0:T(8,128)(2,1)S(1)}, bf16[384,768]{1,0:T(8,128)(2,1)S(1)}, u32[]{:S(2)}, u32[]{:S(2)}) collective-permute-start(bf16[384,768]{1,0:T(8,128)(2,1)S(1)} %add_convert_fusion.4), channel_id=1, source_target_pairs={{0,1},{1,0},{2,3},{3,2},{4,5},{5,4},{6,7},{7,6},{8,9},{9,8},{10,11... | collective-permute-start | bytes 1769480 | tf_op jit(solution)/shard_map/ppermute | solution.py:31
  320.3 22.1 %collective-permute-start.28 = (bf16[96,768]{1,0:T(8,128)(2,1)}, bf16[96,768]{1,0:T(8,128)(2,1)}, u32[]{:S(2)}, u32[]{:S(2)}) collective-permute-start(bf16[96,768]{1,0:T(8,128)(2,1)} %get-tuple-element.229), channel_id=1, source_target_pairs={{0,8},{4,12},{8,16},{12,20},{16,24},{20,28},{24,0},{28,4},{1,9},{5... | collective-permute-start | bytes 442376 | tf_op jit(solution)/shard_map/ppermute | solution.py:85
  320.3 22.1 %collective-permute-start.29 = (bf16[96,768]{1,0:T(8,128)(2,1)}, bf16[96,768]{1,0:T(8,128)(2,1)}, u32[]{:S(2)}, u32[]{:S(2)}) collective-permute-start(bf16[96,768]{1,0:T(8,128)(2,1)} %get-tuple-element.231), channel_id=1, source_target_pairs={{0,16},{4,20},{8,24},{12,28},{16,0},{20,4},{24,8},{28,12},{1,17},{... | collective-permute-start | bytes 442376 | tf_op jit(solution)/shard_map/ppermute | solution.py:85
  322.1 20.2 %collective-permute-start.30 = (bf16[96,768]{1,0:T(8,128)(2,1)}, bf16[96,768]{1,0:T(8,128)(2,1)}, u32[]{:S(2)}, u32[]{:S(2)}) collective-permute-start(bf16[96,768]{1,0:T(8,128)(2,1)} %get-tuple-element.230), channel_id=1, source_target_pairs={{0,24},{4,28},{8,0},{12,4},{16,8},{20,12},{24,16},{28,20},{1,25},{... | collective-permute-start | bytes 442376 | tf_op jit(solution)/shard_map/ppermute | solution.py:85
  336.7 4.3 %collective-permute-start.34 = (f32[10,768]{1,0:T(8,128)}, f32[10,768]{1,0:T(8,128)S(1)}, u32[]{:S(2)}, u32[]{:S(2)}) collective-permute-start(f32[10,768]{1,0:T(8,128)} %stack.66), channel_id=1, source_target_pairs={{0,4},{4,0},{8,12},{12,8},{16,20},{20,16},{24,28},{28,24},{1,5},{5... | collective-permute-start | bytes 92168 | tf_op jit(solution)/shard_map/ppermute | solution.py:31
  341.8 4.1 %collective-permute-start.35 = (f32[10,768]{1,0:T(8,128)S(1)}, f32[10,768]{1,0:T(8,128)S(1)}, u32[]{:S(2)}, u32[]{:S(2)}) collective-permute-start(f32[10,768]{1,0:T(8,128)S(1)} %add.1074), channel_id=1, source_target_pairs={{0,8},{4,12},{8,0},{12,4},{16,24},{20,28},{24,16},{28,20},{1,9},{5... | collective-permute-start | bytes 92168 | tf_op jit(solution)/shard_map/ppermute | solution.py:31
  345.9 5.6 %collective-permute-start.36 = (f32[10,768]{1,0:T(8,128)S(1)}, f32[10,768]{1,0:T(8,128)S(1)}, u32[]{:S(2)}, u32[]{:S(2)}) collective-permute-start(f32[10,768]{1,0:T(8,128)S(1)} %add.1075), channel_id=1, source_target_pairs={{0,16},{4,20},{8,24},{12,28},{16,0},{20,4},{24,8},{28,12},{1,17},{... | collective-permute-start | bytes 92168 | tf_op jit(solution)/shard_map/ppermute | solution.py:31
  348.0 31.7 %copy-start.74 = (f32[192,96]{0,1:T(8,128)S(1)}, f32[192,96]{0,1:T(8,128)}, u32[]{:S(2)}) copy-start(f32[192,96]{0,1:T(8,128)} %copy.171) | copy-start | bytes 221188
  348.0 31.7 %copy-start.75 = (f32[192,96]{0,1:T(8,128)S(1)}, f32[192,96]{0,1:T(8,128)}, u32[]{:S(2)}) copy-start(f32[192,96]{0,1:T(8,128)} %copy.168) | copy-start | bytes 221188
  348.0 31.7 %copy-start.76 = (f32[192,96]{0,1:T(8,128)S(1)}, f32[192,96]{0,1:T(8,128)}, u32[]{:S(2)}) copy-start(f32[192,96]{0,1:T(8,128)} %copy.169) | copy-start | bytes 221188
  350.5 31.8 %copy-start.56 = (f32[96,3,192]{0,2,1:T(8,128)S(1)}, f32[96,3,192]{0,2,1:T(8,128)}, u32[]{:S(2)}) copy-start(f32[96,3,192]{0,2,1:T(8,128)} %copy.167) | copy-start | bytes 663556
  350.5 31.8 %copy-start.57 = (f32[96,3,192]{0,2,1:T(8,128)S(1)}, f32[96,3,192]{0,2,1:T(8,128)}, u32[]{:S(2)}) copy-start(f32[96,3,192]{0,2,1:T(8,128)} %copy.163) | copy-start | bytes 663556
  350.5 31.8 %copy-start.58 = (f32[96,3,192]{0,2,1:T(8,128)S(1)}, f32[96,3,192]{0,2,1:T(8,128)}, u32[]{:S(2)}) copy-start(f32[96,3,192]{0,2,1:T(8,128)} %copy.165) | copy-start | bytes 663556
  351.5 29.9 %copy-start.80 = (f32[10,768]{1,0:T(8,128)}, f32[10,768]{1,0:T(8,128)S(1)}, u32[]{:S(2)}) copy-start(f32[10,768]{1,0:T(8,128)S(1)} %add.1076) | copy-start | bytes 92164
  358.1 3.7 collective-permute-start.31
  362.4 3.6 collective-permute-start.32
  366.6 4.5 %collective-permute-start.33 = (f32[]{:T(128)}, f32[]{:T(128)}, u32[]{:S(2)}, u32[]{:S(2)}) collective-permute-start(f32[]{:T(128)} %add.1053), channel_id=1, source_target_pairs={{0,16},{4,20},{8,24},{12,28},{16,0},{20,4},{24,8},{28,12},{1,17},{... | collective-permute-start | bytes 20 | tf_op jit(solution)/shard_map/ppermute | solution.py:31
  373.0 1.2 collective-permute-start.37
  374.7 3.6 collective-permute-start.38
  (161 other events, 840.8 us)
Sparse Core Ops, SparseCore 0:
  21.6 62.6 all-gather.1
  212.7 67.2 reduce-scatter.3

commit v2 on v1

v2 whole, which is shorter than its diff:
```python
import functools

import jax
import jax.numpy as jnp
from jax import lax
from jax.experimental import pallas as pl
from jax.experimental.pallas import tpu as pltpu
from jax.sharding import PartitionSpec as P

HD = 64
STEP = 5
TILE = 128
BLOCK = 256
CHUNK = 192
REACH = (64, 128)

norm_eps = 1e-05
clip_limit = 1.0
beta_first = 0.5
beta_second = 0.5
adam_eps = 1e-08
matrix_decay = 0.01
masked_score = -1e30
step_rates = (0.03, 0.2, 0.03, 0.015, 0.3, 0.3, 0.3)
bf16 = jnp.bfloat16
f32 = jnp.float32

NN = ((1,), (0,))
NT = ((1,), (1,))
TN = ((0,), (0,))


def dot(a, b, dims):
    return lax.dot_general(a, b, (dims, ((), ())), preferred_element_type=f32)


def shape(dims, dtype):
    return jax.ShapeDtypeStruct(dims, dtype)


def call(body, outs, words, arrays, after=(), limit=16, scratch=()):
    count = len(after)

    def kernel(*refs):
        body(*refs[: len(words)], *refs[len(words) + count :])

    in_vmem = pl.BlockSpec(memory_space=pltpu.VMEM)
    in_specs = [pl.BlockSpec(memory_space=pltpu.SMEM)] * len(words)
    in_specs += [pl.BlockSpec(memory_space=pl.ANY)] * count
    operands = []
    for v in arrays:
        if isinstance(v, tuple):
            v, plane = v
            in_specs.append(pl.BlockSpec((None, *v.shape[1:]), functools.partial(plane_index, plane)))
        else:
            in_specs.append(in_vmem)
        operands.append(v)
    planes = any(isinstance(v, tuple) for v in arrays)
    return pl.pallas_call(
        kernel,
        grid=(1,) if planes else (),
        out_shape=outs,
        in_specs=in_specs,
        out_specs=(in_vmem,) * len(outs) if isinstance(outs, tuple) else in_vmem,
        scratch_shapes=list(scratch),
        compiler_params=pltpu.CompilerParams(vmem_limit_bytes=limit * 2**20),
        cost_estimate=pl.CostEstimate(flops=0, bytes_accessed=0, transcendentals=0),
    )(*words, *after, *operands)


def plane_index(plane, step):
    return (plane, 0, 0)


def core_index():
    return lax.rem(lax.axis_index("tensor"), 2)


def dp_place():
    me = lax.axis_index("dp")
    return lax.div(me, 2), lax.rem(me, 2)


def rows_sum(v):
    return jnp.sum(v, axis=0, keepdims=True)


def whole_sum(v):
    return jnp.sum(rows_sum(v), axis=1, keepdims=True)


def norm_parts(stream):
    center = stream - jnp.mean(stream, axis=-1, keepdims=True)
    spread = jnp.mean(center * center, axis=-1, keepdims=True)
    scale = lax.rsqrt(spread + norm_eps)
    return center * scale, scale


def norm_back(scaled, xhat, scale):
    mean = jnp.mean(scaled, axis=-1, keepdims=True)
    return scale * (scaled - mean - xhat * jnp.mean(scaled * xhat, axis=-1, keepdims=True))


def adamw_step(weight, moment_old, square_old, gradient, step_rate, decay_value, clip_factor):
    correct_one = 1.0 - beta_first**STEP
    correct_two = 1.0 - beta_second**STEP
    clipped = gradient * clip_factor
    moment_new = beta_first * moment_old + (1.0 - beta_first) * clipped
    square_new = beta_second * square_old + (1.0 - beta_second) * clipped * clipped
    divisor = jnp.sqrt(square_new / correct_two) + adam_eps
    weight_new = weight - step_rate * (moment_new / correct_one / divisor + decay_value * weight)
    return (weight_new, moment_new, square_new)


def swap_bit(v, axis, size, bit):
    return lax.ppermute(v, axis, [(i, i ^ bit) for i in range(size)])


def outer_blocks(shard, n):
    outer = n // 2
    blocks = []
    for k in range(1, outer):
        pairs = [(i, ((i // 2 - k) % outer) * 2 + i % 2) for i in range(n)]
        blocks.append(lax.ppermute(shard, "dp", pairs))
    return blocks + [shard]


def dp_sum(v, n):
    bit = 1
    while bit < n:
        v = v + swap_bit(v, "dp", n, bit)
        bit *= 2
    return v


def stack_kernel(*refs):
    r = refs[0].shape[0]
    for j, ref in enumerate(refs[:-1]):
        refs[-1][j * r : (j + 1) * r, :] = ref[...]


def order_kernel(r, own_ref, other_ref, *out_refs):
    mine, inner = dp_place()
    outer = own_ref.shape[0] // r
    for j in range(outer):
        source = lax.rem(mine + 1 + j, outer)
        for ref, side in ((own_ref, inner), (other_ref, 1 - inner)):
            start = pl.multiple_of((source * 2 + side) * r, 16)
            column = 0
            for out_ref in out_refs:
                stop = column + out_ref.shape[1]
                out_ref[pl.ds(start, r), :] = ref[j * r : (j + 1) * r, column:stop]
                column = stop


def stacked(blocks, after):
    r, width = blocks[0].shape
    if r % 16:
        return jnp.concatenate(blocks)
    return call(stack_kernel, shape((len(blocks) * r, width), bf16), (), blocks, after, 8)


def in_order(own, other, n, *widths):
    r, width = own.shape[0] * 2 // n, own.shape[1]
    if r % 16:
        mine, inner = dp_place()
        own, other = (v.reshape(n // 2, r, width) for v in (own, other))
        sides = [jnp.where(inner == 0, own, other), jnp.where(inner == 0, other, own)]
        rows = jnp.roll(jnp.stack(sides, axis=1), mine + 1, axis=0).reshape(n * r, width)
        return tuple(jnp.split(rows, [sum(widths[:i]) for i in range(1, len(widths))], axis=1))
    outs = tuple(shape((n * r, w), bf16) for w in widths)
    return call(functools.partial(order_kernel, r), outs, (), (own, other), (), 8)


def add_kernel(keep_ref, moved_ref, out_ref):
    out_ref[...] = (keep_ref[...].astype(f32) + moved_ref[...].astype(f32)).astype(bf16)


def add(keep, moved, after=()):
    return call(add_kernel, shape(keep.shape, bf16), (), (keep, moved), after, 8)


def over_core(v):
    return swap_bit(v, "tensor", 4, 1)


def over_chip(v):
    return swap_bit(v, "tensor", 4, 2)


def pack_first_kernel(qkv_ref, proj_ref, qk_ref, vp_ref):
    qk_ref[...] = jnp.concatenate([qkv_ref[0], qkv_ref[1]], axis=1).astype(bf16)
    vp_ref[...] = jnp.concatenate([qkv_ref[2], proj_ref[...].T], axis=1).astype(bf16)


def cast_kernel(*refs):
    half = len(refs) // 2
    for source, out in zip(refs[:half], refs[half:]):
        out[...] = source[...].astype(bf16)


def segment_grid(lengths_ref, dims, axis):
    places = lax.broadcasted_iota(jnp.int32, dims, axis)
    ids = jnp.zeros(dims, jnp.int32)
    bound = jnp.int32(0)
    for k in range(lengths_ref.shape[1]):
        bound = bound + lengths_ref[0, k]
        ids = ids + (places >= bound).astype(jnp.int32)
    return ids


def valid_count(lengths_ref):
    total = jnp.int32(0)
    for k in range(lengths_ref.shape[1]):
        total = total + lengths_ref[0, k]
    return total


def first_norm_kernel(lengths_one, lengths_two, inputs_ref, times_one, times_two, vecs_ref, *refs):
    rows = inputs_ref.shape[1]
    for b, (lengths_ref, times_ref) in enumerate(((lengths_one, times_one), (lengths_two, times_two))):
        stream_ref, normed_ref = refs[2 * b : 2 * b + 2]
        depth = times_ref.shape[0]
        ids = segment_grid(lengths_ref, (rows, 1), 0)
        for start in range(0, rows, BLOCK):
            here = slice(start, start + BLOCK)
            lanes = lax.broadcasted_iota(jnp.int32, (BLOCK, depth), 1)
            pick = (ids[here] == lanes).astype(f32).astype(bf16)
            stream = inputs_ref[b, here, :].astype(f32) + dot(pick, times_ref[...], NN)
            stream_ref[here, :] = stream
            xhat, _ = norm_parts(stream)
            normed_ref[here, :] = (xhat * vecs_ref[0:1, :] + vecs_ref[1:2, :]).astype(bf16)


def windows(rows, reach):
    size = min(rows, TILE + 2 * reach)
    out = []
    for start in range(0, rows, TILE):
        low = max(0, start - reach)
        high = min(rows, start + TILE + reach)
        if (high - low) % 128:
            low = min(low, rows - size)
            high = low + size
        out.append((start, low, high))
    return out


def split_heads(low, rows, q_s, k_s, v_s):
    heads = q_s.shape[0]
    width = heads * HD
    for h in range(heads):
        cut = h * HD
        q_s[h, rows, :] = low[:, cut : cut + HD] * jnp.array(HD**-0.5, bf16)
        k_s[h, rows, :] = low[:, width + cut : width + cut + HD]
        v_s[h, rows, :] = low[:, 2 * width + cut : 2 * width + cut + HD]


def forward_kernel(reach, lengths_ref, normed_ref, qk_ref, wv_ref, bias_ref, att_ref, qkv_ref, lse_ref, q_s, k_s, v_s):
    rows, width = att_ref.shape
    heads = range(width // HD)
    for start in range(0, rows, BLOCK):
        piece = slice(start, start + BLOCK)
        normed = normed_ref[piece, :]
        pair = dot(normed, qk_ref[...], NN)
        values = dot(normed, wv_ref[...], NN)
        low = (jnp.concatenate([pair, values], axis=1) + bias_ref[...]).astype(bf16)
        qkv_ref[piece, :] = low
        split_heads(low, piece, q_s, k_s, v_s)
    ids_col = segment_grid(lengths_ref, (rows, 1), 0)
    ids_row = segment_grid(lengths_ref, (1, rows), 1)
    lanes = lax.broadcasted_iota(jnp.int32, (TILE, 128), 1)
    for start, low, high in windows(rows, reach):
        tile = slice(start, start + TILE)
        allowed = ids_col[tile] == ids_row[:, low:high]
        scores = [dot(q_s[h, tile, :], k_s[h, low:high, :], NT) for h in heads]
        scores = [jnp.where(allowed, s, masked_score) for s in scores]
        peaks = [jnp.max(s, axis=-1, keepdims=True) for s in scores]
        exponents = [jnp.exp(s - p) for s, p in zip(scores, peaks)]
        totals = [jnp.sum(e, axis=-1, keepdims=True) for e in exponents]
        probs = [(e * (1.0 / t)).astype(bf16) for e, t in zip(exponents, totals)]
        outs = [dot(p, v_s[h, low:high, :], NN).astype(bf16) for h, p in enumerate(probs)]
        att_ref[tile, :] = jnp.concatenate(outs, axis=1)
        logs = jnp.zeros((TILE, 128), f32)
        for h in heads:
            logs = jnp.where(lanes == h, peaks[h] + jnp.log(totals[h]), logs)
        lse_ref[tile, :] = logs


def hidden_kernel(lengths_ref, *refs):
    att_refs, proj_refs = refs[:4], refs[4:8]
    stream_ref, vecs_ref, up_ref, down_ref, bias_ref, cot_ref = refs[8:14]
    middle_ref, normed_ref, active_ref, upstream_ref, grad_ref, away_ref, keep_ref, square_ref, offset_ref = refs[14:]
    rows, features = stream_ref.shape
    half = rows // 2
    core = core_index()
    total = valid_count(lengths_ref)
    squares = jnp.zeros((1, features), f32)
    offsets = jnp.zeros((1, grad_ref.shape[1]), f32)
    for out_ref, base in ((away_ref, (1 - core) * half), (keep_ref, core * half)):
        for start in range(0, half, CHUNK):
            off = pl.multiple_of(base + start, CHUNK)
            here = pl.ds(off, CHUNK)
            valid = off + lax.broadcasted_iota(jnp.int32, (CHUNK, 1), 0) < total
            upstream = jnp.where(valid, cot_ref[here, :].astype(f32), 0.0).astype(bf16)
            upstream_ref[here, :] = upstream
            own, near, over, across = (dot(a[here, :], p[...], NT) for a, p in zip(att_refs, proj_refs))
            branch = ((own + near) + (over + across)) + vecs_ref[4:5, :]
            kept = jnp.where(valid, branch, 0.0)
            squares = squares + rows_sum(kept * kept)
            middle = stream_ref[here, :] + branch
            middle_ref[here, :] = middle
            xhat, _ = norm_parts(middle)
            normed = (xhat * vecs_ref[2:3, :] + vecs_ref[3:4, :]).astype(bf16)
            normed_ref[here, :] = normed
            hidden = dot(normed, up_ref[...], NN) + bias_ref[...]
            cdf = 0.5 + 0.5 * lax.erf(hidden * 0.5**0.5)
            pdf = jnp.exp(-0.5 * hidden * hidden) * 0.3989422804014327
            active_ref[here, :] = (hidden * cdf).astype(bf16)
            grad = dot(upstream, down_ref[...], NN) * (cdf + hidden * pdf)
            offsets = offsets + rows_sum(grad)
            low = grad.astype(bf16)
            grad_ref[here, :] = low
            out_ref[start : start + CHUNK, :] = dot(low, up_ref[...], NT).astype(out_ref.dtype)
    square_ref[...] = squares
    offset_ref[...] = offsets


def down_kernel(active_ref, down_ref, away_ref, keep_ref):
    half = active_ref.shape[0] // 2
    core = core_index()
    for out_ref, base in ((away_ref, (1 - core) * half), (keep_ref, core * half)):
        here = pl.ds(pl.multiple_of(base, half), half)
        out_ref[...] = dot(active_ref[here, :], down_ref[...], NT).astype(out_ref.dtype)


def products_kernel(pairs, *refs):
    out_ref = refs[-1]
    for m in range(0, out_ref.shape[0], BLOCK):
        cut = slice(m, m + BLOCK)
        column = 0
        for p in range(pairs):
            left_one, left_two, right_one, right_two = refs[4 * p : 4 * p + 4]
            part = dot(left_one[:, cut], right_one[...], TN) + dot(left_two[:, cut], right_two[...], TN)
            out_ref[cut, column : column + part.shape[1]] = part.astype(out_ref.dtype)
            column += part.shape[1]


def parted_kernel(r, *refs):
    away_ref, keep_ref, full_s = refs[-3:]
    products_kernel(len(refs) // 4, *refs[:-3], full_s)
    _, inner = dp_place()
    for o in range(away_ref.shape[0] // r):
        for out_ref, side in ((away_ref, 1 - inner), (keep_ref, inner)):
            start = pl.multiple_of((o * 2 + side) * r, 8)
            out_ref[o * r : (o + 1) * r, :] = full_s[pl.ds(start, r), :].astype(bf16)


def parted(arrays, n, after):
    rows, width = arrays[0].shape[1], sum(v.shape[1] for v in arrays[2::4])
    r = rows // n
    if r % 16:
        kernel = functools.partial(products_kernel, len(arrays) // 4)
        full = call(kernel, shape((rows, width), bf16), (), arrays, after)
        view = full.reshape(n // 2, 2, r, width)
        _, inner = dp_place()
        pieces = [lax.dynamic_index_in_dim(view, i, 1, False) for i in (1 - inner, inner)]
        return [v.reshape(rows // 2, width) for v in pieces]
    outs = (shape((rows // 2, width), bf16),) * 2
    scratch = [pltpu.VMEM((rows, width), f32)]
    return call(functools.partial(parted_kernel, r), outs, (), arrays, after, 24, scratch)


def blocks_kernel(r, keep_ref, moved_ref, own_ref, *out_refs):
    mine, _ = dp_place()
    outer = keep_ref.shape[0] // r
    for k, out_ref in enumerate((own_ref, *out_refs)):
        here = pl.ds(pl.multiple_of(lax.rem(mine + k, outer) * r, 16), r)
        total = keep_ref[here, :].astype(f32) + moved_ref[here, :].astype(f32)
        out_ref[...] = total.astype(out_ref.dtype)


def scattered(away, keep, n, after):
    outer, width = n // 2, keep.shape[1]
    r = keep.shape[0] // outer
    moved = swap_bit(away, "dp", n, 1)
    if r % 16:
        mine, _ = dp_place()
        total = (keep.astype(f32) + moved.astype(f32)).reshape(outer, r, width)
        own, *sent = (lax.dynamic_index_in_dim(total, lax.rem(mine + k, outer), 0, False) for k in range(outer))
        sent = [v.astype(bf16) for v in sent]
    else:
        outs = (shape((r, width), f32),) + (shape((r, width), bf16),) * (outer - 1)
        own, *sent = call(functools.partial(blocks_kernel, r), outs, (), (keep, moved), after, 8)
    blocks = [own]
    for k in range(1, outer):
        pairs = [(i, ((i // 2 + k) % outer) * 2 + i % 2) for i in range(n)]
        blocks.append(lax.ppermute(sent[k - 1], "dp", pairs))
    return blocks


def backward_kernel(
    reach,
    lengths_ref,
    both_ref,
    other_ref,
    middle_ref,
    upstream_ref,
    vecs_ref,
    qk_ref,
    wv_ref,
    proj_ref,
    qkv_ref,
    lse_ref,
    grad_middle_ref,
    low_ref,
    mixed_ref,
    away_ref,
    keep_ref,
    sums_ref,
    heads_ref,
    q_s,
    k_s,
    v_s,
    g_s,
    dk_s,
    dv_s,
):
    rows, features = middle_ref.shape
    half = rows // 2
    width = qkv_ref.shape[1] // 3
    heads = range(width // HD)
    core = core_index()
    ids_col = segment_grid(lengths_ref, (rows, 1), 0)
    ids_row = segment_grid(lengths_ref, (1, rows), 1)
    gain = vecs_ref[2:3, :]
    sums = []
    for piece_ref, base in ((both_ref, core * half), (other_ref, (1 - core) * half)):

        def rows_step(t, acc, piece_ref=piece_ref, base=base):
            off = pl.multiple_of(base + t * TILE, TILE)
            here = pl.ds(off, TILE)
            gnt = piece_ref[pl.ds(pl.multiple_of(t * TILE, TILE), TILE), :].astype(f32)
            xhat, scale = norm_parts(middle_ref[here, :])
            upstream = upstream_ref[here, :].astype(f32)
            grad_middle = upstream + norm_back(gnt * gain, xhat, scale)
            grad_middle_ref[here, :] = grad_middle
            low_ref[here, :] = grad_middle.astype(bf16)
            terms = (gnt * xhat, gnt, grad_middle, upstream)
            return tuple(a + rows_sum(v) for a, v in zip(acc, terms))

        start = (jnp.zeros((1, features), f32),) * 4
        sums.append(lax.fori_loop(0, half // TILE, rows_step, start))
    sums_ref[...] = jnp.concatenate([a + b for a, b in zip(*sums)], axis=0)
    for start in range(0, rows, BLOCK):
        piece = slice(start, start + BLOCK)
        split_heads(qkv_ref[piece, :], piece, q_s, k_s, v_s)
        grad_att = dot(low_ref[piece, :], proj_ref[...], NN).astype(bf16)
        for h in heads:
            g_s[h, piece, :] = grad_att[:, h * HD : (h + 1) * HD]
    dk_s[...] = jnp.zeros_like(dk_s)
    dv_s[...] = jnp.zeros_like(dv_s)
    for start, low, high in windows(rows, reach):
        tile = slice(start, start + TILE)
        keys = slice(low, high)
        allowed = ids_col[tile] == ids_row[:, keys]
        scores = [dot(q_s[h, tile, :], k_s[h, keys, :], NT) for h in heads]
        grad_probs = [dot(g_s[h, tile, :], v_s[h, keys, :], NT) for h in heads]
        probs = [jnp.exp(jnp.where(allowed, s, masked_score) - lse_ref[tile, h : h + 1]) for h, s in enumerate(scores)]
        inner = [jnp.sum(p * g, axis=-1, keepdims=True) for p, g in zip(probs, grad_probs)]
        grads = [(p * (g - i)).astype(bf16) for p, g, i in zip(probs, grad_probs, inner)]
        lows = [p.astype(bf16) for p in probs]
        dqs = [(dot(g, k_s[h, keys, :], NN) * HD**-0.5).astype(bf16) for h, g in enumerate(grads)]
        mixed_ref[tile, :width] = jnp.concatenate(dqs, axis=1)
        dks = [dot(g, q_s[h, tile, :], TN) for h, g in enumerate(grads)]
        dvs = [dot(p, g_s[h, tile, :], TN) for h, p in enumerate(lows)]
        for h in heads:
            dk_s[h, keys, :] += dks[h]
            dv_s[h, keys, :] += dvs[h]
    for start in range(0, rows, BLOCK):
        piece = slice(start, start + BLOCK)
        both = [ref[h, piece, :].astype(bf16) for ref in (dk_s, dv_s) for h in heads]
        mixed_ref[piece, width:] = jnp.concatenate(both, axis=1)
    heads_ref[...] = rows_sum(mixed_ref[...].astype(f32))
    for out_ref, base in ((away_ref, (1 - core) * half), (keep_ref, core * half)):
        here = pl.ds(pl.multiple_of(base, half), half)
        part = dot(mixed_ref[here, : 2 * width], qk_ref[...], NT)
        part = part + dot(mixed_ref[here, 2 * width :], wv_ref[...], NT)
        out_ref[...] = part.astype(out_ref.dtype)


def input_grad_kernel(both_ref, other_ref, stream_ref, middle_ref, vecs_ref, *refs):
    out_ref, sums_ref = refs[-2:]
    rows, features = stream_ref.shape
    half = rows // 2
    core = core_index()
    gain = vecs_ref[0:1, :]
    sums = []
    for piece_ref, base in ((both_ref, core * half), (other_ref, (1 - core) * half)):

        def rows_step(t, acc, piece_ref=piece_ref, base=base):
            here = pl.ds(pl.multiple_of(base + t * TILE, TILE), TILE)
            grad = piece_ref[pl.ds(pl.multiple_of(t * TILE, TILE), TILE), :].astype(f32)
            xhat, scale = norm_parts(stream_ref[here, :])
            out_ref[0, here, :] = middle_ref[here, :] + norm_back(grad * gain, xhat, scale)
            return (acc[0] + rows_sum(grad * xhat), acc[1] + rows_sum(grad))

        start = (jnp.zeros((1, features), f32),) * 2
        sums.append(lax.fori_loop(0, half // TILE, rows_step, start))
    sums_ref[...] = jnp.concatenate([a + b for a, b in zip(*sums)], axis=0)


def input_grad_call(which, both, other, stream, middle, vecs, filled, after):
    rows, features = stream.shape
    count = len(after)

    def kernel(*refs):
        input_grad_kernel(*refs[count:])

    whole = pl.BlockSpec(memory_space=pltpu.VMEM)
    anywhere = pl.BlockSpec(memory_space=pl.ANY)
    return pl.pallas_call(
        kernel,
        grid=(1,),
        out_shape=(shape((2, rows, features), f32), shape((2, features), f32)),
        in_specs=[anywhere] * count + [whole] * 5 + [anywhere] * len(filled),
        out_specs=(pl.BlockSpec((1, rows, features), lambda i: (which, 0, 0)), whole),
        input_output_aliases={count + 5: 0} if filled else {},
        compiler_params=pltpu.CompilerParams(vmem_limit_bytes=24 * 2**20),
        cost_estimate=pl.CostEstimate(flops=0, bytes_accessed=0, transcendentals=0),
    )(*after, both, other, stream, middle, vecs, *filled)


def output_kernel(lengths_one, lengths_two, *refs):
    vecs_ref, branch_one, branch_two, out_ref, sums_ref = refs[6:]
    features = out_ref.shape[2]
    half = out_ref.shape[1] // 2
    core = core_index()
    sums = []
    count = jnp.int32(0)
    for b, lengths_ref in enumerate((lengths_one, lengths_two)):
        total = valid_count(lengths_ref)
        count = count + total
        both_ref, other_ref, middle_ref = refs[3 * b : 3 * b + 3]
        for piece_ref, base in ((both_ref, core * half), (other_ref, (1 - core) * half)):

            def rows_step(t, acc, piece_ref=piece_ref, base=base, middle_ref=middle_ref, total=total, b=b):
                off = pl.multiple_of(base + t * TILE, TILE)
                here = pl.ds(off, TILE)
                two = piece_ref[pl.ds(pl.multiple_of(t * TILE, TILE), TILE), :].astype(f32) + vecs_ref[5:6, :]
                whole = middle_ref[here, :] + two
                out_ref[b, here, :] = whole.astype(bf16)
                valid = off + lax.broadcasted_iota(jnp.int32, (TILE, 1), 0) < total
                terms = [jnp.where(valid, v, 0.0) for v in (whole, two)]
                return tuple(a + rows_sum(v * v) for a, v in zip(acc, terms))

            start = (jnp.zeros((1, features), f32),) * 2
            sums.append(lax.fori_loop(0, half // TILE, rows_step, start))
    whole, two = ((a + b) + (c + d) for a, b, c, d in zip(*sums))
    lines = [jnp.sum(v, axis=1, keepdims=True) for v in (whole, branch_one[...] + branch_two[...], two)]
    lines.append(jnp.full((1, 1), count.astype(f32), f32))
    for i in range(8):
        sums_ref[i : i + 1, :] = jnp.broadcast_to(lines[min(i, 3)], (1, 128))


def message_kernel(*refs):
    out_ref, grads_ref = refs[-2:]
    norm_one, norm_two, sums_one, sums_two, off_one, off_two, heads_one, heads_two = refs[-10:-2]
    block_refs = refs[:-10]
    count = len(block_refs) // 2
    width = heads_one.shape[1] // 3
    column = 0
    squares = jnp.zeros((1, 1), f32)
    for group in (block_refs[:count], block_refs[count:]):
        grad = group[0][...]
        for ref in group[1:]:
            grad = grad + ref[...].astype(f32)
        stop = column + grad.shape[1]
        grads_ref[:, column:stop] = grad
        squares = squares + whole_sum(grad * grad)
        column = stop
    out_ref[...] = jnp.zeros_like(out_ref)
    out_ref[0:2, :] = norm_one[...] + norm_two[...]
    out_ref[2:6, :] = sums_one[...] + sums_two[...]
    out_ref[6:7, :] = off_one[...] + off_two[...]
    heads = heads_one[...] + heads_two[...]
    out_ref[8:9, :width] = heads[:, :width]
    out_ref[9:10, :width] = heads[:, 2 * width :]
    out_ref[10:11, :] = jnp.broadcast_to(squares, (1, out_ref.shape[1]))


def partial_kernel(message_ref, out_ref):
    squares = whole_sum(message_ref[8:10, :] * message_ref[8:10, :])
    squares = squares + whole_sum(message_ref[6:7, :] * message_ref[6:7, :])
    out_ref[...] = jnp.broadcast_to(squares + message_ref[10:11, 0:1], out_ref.shape)


def adamw_kernel(partial_ref, moved_ref, message_ref, grads_ref, *refs):
    count = 21
    sources, targets, norm_ref = refs[:count], refs[count : 2 * count], refs[2 * count]
    inputs, outputs = refs[2 * count + 1 : 3 * count + 1], refs[3 * count + 1 : 4 * count + 1]
    read_sems, write_sems = refs[4 * count + 1 :]
    reads = [pltpu.make_async_copy(sources[i], inputs[i], read_sems.at[i]) for i in range(count)]
    writes = [pltpu.make_async_copy(outputs[i], targets[i], write_sems.at[i]) for i in range(count)]
    for copy in reads:
        copy.start()
    width = inputs[0].shape[2]
    hidden = inputs[6].shape[1]
    vecs = message_ref[0:6, :]
    norm = jnp.sqrt(partial_ref[0:1, 0:1] + moved_ref[0:1, 0:1] + whole_sum(vecs * vecs))
    norm_ref[...] = jnp.broadcast_to(norm, norm_ref.shape)
    clip = jnp.minimum(1.0, clip_limit / (norm + 1e-06))

    def step(p, gradient, at=Ellipsis):
        weight, moment, square = (ref[at] for ref in inputs[3 * p : 3 * p + 3])
        decay = matrix_decay if p < 4 else 0.0
        values = adamw_step(weight, moment, square, gradient, step_rates[p], decay, clip)
        for ref, value in zip(outputs[3 * p : 3 * p + 3], values):
            ref[at] = value

    start = 4 * width
    parts = (
        tuple((grads_ref[:, j * width : (j + 1) * width], j) for j in range(3)),
        ((grads_ref[:, 3 * width : start].T,),),
        ((grads_ref[:, start : start + hidden],),),
        ((grads_ref[:, start + hidden :],),),
        ((vecs,),),
        ((message_ref[8:10, : inputs[15].shape[1]],),),
        ((message_ref[6:7, :],),),
    )
    for p, steps in enumerate(parts):
        for copy in reads[3 * p : 3 * p + 3]:
            copy.wait()
        for arguments in steps:
            step(p, *arguments)
        for copy in writes[3 * p : 3 * p + 3]:
            copy.start()
    for copy in writes:
        copy.wait()


def adamw_call(partial, moved, message, grads, state):
    in_vmem = pl.BlockSpec(memory_space=pltpu.VMEM)
    anywhere = pl.BlockSpec(memory_space=pltpu.MemorySpace.HBM)
    count = len(state)
    return pl.pallas_call(
        adamw_kernel,
        out_shape=tuple(shape(v.shape, f32) for v in state) + (shape((1, 128), f32),),
        in_specs=[in_vmem] * 4 + [anywhere] * count,
        out_specs=(anywhere,) * count + (in_vmem,),
        scratch_shapes=[pltpu.VMEM(v.shape, f32) for v in state] * 2 + [pltpu.SemaphoreType.DMA((count,))] * 2,
        compiler_params=pltpu.CompilerParams(vmem_limit_bytes=24 * 2**20),
        cost_estimate=pl.CostEstimate(flops=10**7, bytes_accessed=10**7, transcendentals=0),
    )(partial, moved, message, grads, *state)


def build(n):
    def local(
        inputs,
        time_first,
        time_second,
        lengths_first,
        lengths_second,
        cotangent,
        w_qkv,
        m_qkv,
        v_qkv,
        w_proj,
        m_proj,
        v_proj,
        w_up,
        m_up,
        v_up,
        w_down,
        m_down,
        v_down,
        w_vecs,
        m_vecs,
        v_vecs,
        b_heads,
        m_heads,
        v_heads,
        b_hidden,
        m_hidden,
        v_hidden,
    ):
        rows, features = inputs.shape[1], inputs.shape[2]
        r, _, width = w_qkv.shape
        hidden = w_up.shape[1]
        heads = width // HD
        half = rows // 2
        lengths = (lengths_first, lengths_second)
        whole_f = shape((rows, features), f32)
        whole_b = shape((rows, features), bf16)
        half_b = shape((half, features), bf16)
        half_f = shape((half, features), f32)
        line = shape((1, features), f32)

        qkv_planes = w_qkv.transpose(1, 0, 2)
        qk_shard, vp_shard = call(
            pack_first_kernel, (shape((r, 2 * width), bf16),) * 2, (), (qkv_planes, w_proj), (), 8
        )
        qk_blocks, vp_blocks = outer_blocks(qk_shard, n), outer_blocks(vp_shard, n)
        stream_one, normed_one, stream_two, normed_two = call(
            first_norm_kernel,
            (whole_f, whole_b) * 2,
            lengths,
            (inputs, *(jnp.pad(t[0], ((0, 16 - t.shape[1]), (0, 0))) for t in (time_first, time_second)), w_vecs),
            (qk_shard,),
            24,
        )
        stream, normed = (stream_one, stream_two), (normed_one, normed_two)
        qk_own = stacked(qk_blocks, (normed_two,))
        qk_other = swap_bit(qk_own, "dp", n, 1)
        up_shard, down_shard = call(
            cast_kernel, (shape((r, hidden), bf16),) * 2, (), (w_up, w_down.T), (qk_own,), 8
        )
        up_blocks = outer_blocks(up_shard, n)
        vp_own = stacked(vp_blocks, (up_shard,))
        vp_other = swap_bit(vp_own, "dp", n, 1)
        down_blocks = outer_blocks(down_shard, n)
        (qk,) = in_order(qk_own, qk_other, n, 2 * width)
        wv, proj_own = in_order(vp_own, vp_other, n, width, width)

        def spread(v):
            moved = over_chip(v)
            return [v, over_core(v), moved, over_core(moved)]

        proj = spread(proj_own)
        bias = jnp.concatenate([b_heads[0], jnp.zeros_like(b_heads[0]), b_heads[1]])[None]
        head_low = pltpu.VMEM((heads, rows, HD), bf16)
        head_full = pltpu.VMEM((heads, rows, HD), f32)

        after = (proj_own,)
        att, qkv, lse, att_all = [], [], [], []
        for b in range(2):
            a, q, l = call(
                functools.partial(forward_kernel, REACH[b]),
                (shape((rows, width), bf16), shape((rows, 3 * width), bf16), shape((rows, 128), f32)),
                (lengths[b],),
                (normed[b], qk, wv, bias),
                after,
                12,
                [head_low] * 3,
            )
            att.append(a)
            qkv.append(q)
            lse.append(l)
            att_all.append(spread(a))
            if b == 0:
                up_own = stacked(up_blocks, (l,))
                up_other = swap_bit(up_own, "dp", n, 1)
                down_own = stacked(down_blocks, (up_own,))
                down_other = swap_bit(down_own, "dp", n, 1)
                after = (down_own, proj[2])
        (up,) = in_order(up_own, up_other, n, hidden)
        (down,) = in_order(down_own, down_other, n, hidden)
        after = (lse[1], att_all[0][2])

        names = [[] for _ in range(9)]
        low = []
        for b in range(2):
            outs = call(
                hidden_kernel,
                (
                    whole_f,
                    whole_b,
                    shape((rows, hidden), bf16),
                    whole_b,
                    shape((rows, hidden), bf16),
                    half_b,
                    half_f,
                    line,
                    shape((1, hidden), f32),
                ),
                (lengths[b],),
                (*att_all[b], *proj, stream[b], w_vecs, up, down, b_hidden[None], (cotangent, b)),
                after,
                20,
            )
            for kept, v in zip(names, outs):
                kept.append(v)
            low.append(add(outs[6], over_core(outs[5]), (outs[-1],)))
            after = (low[b],)
        middle, normed_mid, active, upstream, grad_hidden, away, keep, branch_square, offsets = names

        bulk = parted((*normed_mid, *grad_hidden, *upstream, *active), n, after)
        after = (bulk[0],)
        parts = []
        for b in range(2):
            parts.append(call(down_kernel, (half_b, half_f), (), (active[b], down), after))
            after = (parts[b][0],)
        gnt = []
        for b in range(2):
            both = add(low[b], over_chip(low[b]), after if b == 0 else ())
            gnt.append((both, over_core(both)))
        after = (gnt[0][0],)

        grad_middle, middle_low, grad_mixed, sums, head_sums, back_low = [], [], [], [], [], []
        for b in range(2):
            outs = call(
                functools.partial(backward_kernel, REACH[b]),
                (
                    whole_f,
                    whole_b,
                    shape((rows, 3 * width), bf16),
                    half_b,
                    half_f,
                    shape((4, features), f32),
                    shape((1, 3 * width), f32),
                ),
                (lengths[b],),
                (*gnt[b], middle[b], upstream[b], w_vecs, qk, wv, proj_own, qkv[b], lse[b]),
                after,
                24,
                [head_low] * 4 + [head_full] * 2,
            )
            grad_middle.append(outs[0])
            middle_low.append(outs[1])
            grad_mixed.append(outs[2])
            sums.append(outs[5])
            head_sums.append(outs[6])
            back_low.append(add(outs[4], over_core(outs[3])))
            after = (back_low[b],)

        bulk_grads = scattered(*bulk, n, after)
        first = parted((*normed, *grad_mixed, *middle_low, *att), n, (bulk_grads[0],))
        both = add(back_low[0], over_chip(back_low[0]), (first[0],))
        pieces = [(both, over_core(both))]
        first_grads = scattered(*first, n, (both,))
        both = add(back_low[1], over_chip(back_low[1]), (first_grads[0],))
        pieces.append((both, over_core(both)))
        after = (first_grads[0],)

        filled, norm_sums = (), []
        for b in range(2):
            grad, pair = input_grad_call(
                b, *pieces[b], stream[b], grad_middle[b], w_vecs, filled, after
            )
            filled = (grad,)
            norm_sums.append(pair)
            after = (pair,)
        input_grad = filled[0]

        two = []
        for b in range(2):
            part = add(parts[b][1], over_core(parts[b][0]), (first[0],) if b == 0 else (first_grads[0],))
            both = add(part, over_chip(part))
            two += [both, over_core(both), middle[b]]
        message, grads = call(
            message_kernel,
            (shape((16, features), f32), shape((r, 4 * width + 2 * hidden), f32)),
            (),
            (*first_grads, *bulk_grads, *norm_sums, *sums, *offsets, *head_sums),
            (),
            16,
        )
        block_out, out_sums = call(
            output_kernel,
            (shape((2, rows, features), bf16), shape((8, 128), f32)),
            lengths,
            (*two, w_vecs, *branch_square),
            (message,),
        )
        message = dp_sum(message, n)
        partial = call(partial_kernel, shape((8, 128), f32), (), (message,), (), 8)
        partial = partial + over_core(partial)
        state = (
            *(v.transpose(1, 0, 2) for v in (w_qkv, m_qkv, v_qkv)),
            *(w_proj, m_proj, v_proj),
            *(w_up, m_up, v_up),
            *(v.T for v in (w_down, m_down, v_down)),
            *(w_vecs, m_vecs, v_vecs),
            *(b_heads, m_heads, v_heads),
            *(b_hidden[None], m_hidden[None], v_hidden[None]),
        )
        *updated, grad_norm = adamw_call(partial, over_chip(partial), message, grads, state)
        out_sums = dp_sum(out_sums, n)
        return (
            block_out,
            input_grad,
            grad_norm[0, :1],
            jnp.sqrt(out_sums[:3, 0] / (out_sums[3, 0] * features)),
            *(v.transpose(1, 0, 2) for v in updated[:3]),
            *updated[3:9],
            *(v.T for v in updated[9:12]),
            *updated[12:18],
            *(v.reshape(hidden) for v in updated[18:]),
        )

    return local


def solution(mesh):
    rows = P(None, "dp", None)
    group = P("dp", None, None)
    qkv, proj, up = P("dp", None, "tensor"), P("tensor", "dp"), P("dp", "tensor")
    params = [qkv] * 3 + [proj] * 3 + [up] * 3 + [proj] * 3 + [P()] * 3
    params += [P(None, "tensor")] * 3 + [P("tensor")] * 3
    return jax.shard_map(
        build(mesh.shape["dp"]),
        mesh=mesh,
        in_specs=(rows, group, group, P("dp", None), P("dp", None), rows, *params),
        out_specs=(rows, rows, P(), P(), *params),
        check_vma=False,
    )
```

time: 404 us -> 276 us (0.68)
  other arithmetic: 93.8 us -> 2.57 us
  Pallas kernels: 0 us -> 85.4 us
  matrix products: 67.2 us -> 0 us
  local copies, waits for them, and re-layouts: 66.5 us -> 11.7 us
  between operations: 42.9 us -> 2.58 us
  starting transfers between devices: 39.5 us -> 73.1 us
  waiting for transfers between devices: 88.6 us -> 96.6 us
    pallas_call x0 -> x41, Pallas kernels: none -> 85.4 us  [the longest x38 73.9 us: call(): pl.pallas_call(kernel, grid=(1,) if planes else (), out_shape=outs, in_sp...]
    dot_general x58 -> x0, matrix products: 67.2 us -> none  [dot(): return lax.dot_general(a, b, (dims, ((), ())), preferred_element_type=f32)]
    reduce_sum x28 -> x0, other arithmetic: 48.8 us -> none  [the longest x2 11 us: local(): s['gain_two'] = jnp.sum(gnt * xhat, axis=0)]
    ppermute x3 -> x18, starting transfers between devices: 3.83 us -> 40.4 us  [the longest x12 27.8 us: outer_blocks(): blocks.append(lax.ppermute(shard, 'dp', pairs))]
    unnamed x383 -> x76, local copies, waits for them, and re-layouts: 42.8 us -> 9.66 us
    convert_element_type x30 -> x0, other arithmetic: 22.1 us -> none  [the longest x6 6.16 us: tensor_sum(): low = (keep + swap_bit(away, 'tensor', 4, 1).astype(f32)).astype(bf16)]
    all_to_all x1 -> x0, waiting for transfers between devices: 12.6 us -> none  [local(): lax.all_to_all(jnp.tile(first_shard, (n, 1)), 'dp', 0, 0, tiled=True)]
    ppermute x3 -> x18, waiting for transfers between devices: 0.01 us -> 11.2 us  [the longest x6 7.09 us: scattered(): blocks.append(lax.ppermute(sent[k - 1], 'dp', pairs))]
  transfers between devices with their start and end apart: 42 -> 59, of which waited for: 16 -> 21; matrix products, arithmetic and copies ran while one was open for 45% -> 1% of each run, Pallas kernels for 0% -> 24%
where the time goes in v2:
time: 276 us; the launch traced here: 272 us
  waiting for transfers between devices  96.6 us (35%)
  Pallas kernels  85.4 us (31%)
  starting transfers between devices  73.1 us (26%)
  local copies, waits for them, and re-layouts  11.7 us (4%)
    ppermute x41, waiting for transfers between devices, swap_bit(): return lax.ppermute(v, axis, [(i, i ^ bit) for i in range(size)])  85.4 us
    pallas_call x38, Pallas kernels, call(): pl.pallas_call(kernel, grid=(1,) if planes else (), out_shape=outs, in_sp...  73.9 us
    ppermute x41, starting transfers between devices, swap_bit(): return lax.ppermute(v, axis, [(i, i ^ bit) for i in range(size)])  32.7 us
    ppermute x12, starting transfers between devices, outer_blocks(): blocks.append(lax.ppermute(shard, 'dp', pairs))  27.8 us
    ppermute x6, starting transfers between devices, scattered(): blocks.append(lax.ppermute(sent[k - 1], 'dp', pairs))  12.6 us
    unnamed x76, local copies, waits for them, and re-layouts  9.66 us
    pallas_call x2, Pallas kernels, input_grad_call(): pl.pallas_call(kernel, grid=(1,), out_shape=(shape((2, rows, features), f...  7.35 us
    ppermute x6, waiting for transfers between devices, scattered(): blocks.append(lax.ppermute(sent[k - 1], 'dp', pairs))  7.09 us
  transfers between devices with their start and end apart: 59, of which 21 were waited for; matrix products, arithmetic and copies ran while one was open for 1% of the time, Pallas kernels for 24%

profile of v2, /device:TPU:0, one launch (start us, length us, event | category | flops | bytes accessed | tf_op | source)
XLA Modules:
  0.0 271.9 jit_solution(4145798617472894087)
XLA Ops:
  0.7 1.0 copy-done.8
  1.6 0.9 copy-done.16
  2.7 5.1 %collective-permute-start = (bf16[96,384]{1,0:T(8,128)(2,1)S(1)}, bf16[96,384]{1,0:T(8,128)(2,1)S(1)}, u32[]{:S(2)}, u32[]{:S(2)}) collective-permute-start(bf16[96,384]{1,0:T(8,128)(2,1)S(1)} %get-tuple-element.119.refs_2_.refs_4_), channel_id=1, source_target_pairs={{0,24},{4,28},{8,0},{12,4},{16,8},{20,12},{24,16},{28,20},{1,25},{... | collective-permute-start | bytes 221192 | tf_op jit(solution)/shard_map/ppermute | solution.py:124
  7.8 1.0 collective-permute-start.2
  8.8 2.8 %collective-permute-start.3 = (bf16[96,384]{1,0:T(8,128)(2,1)S(1)}, bf16[96,384]{1,0:T(8,128)(2,1)S(1)}, u32[]{:S(2)}, u32[]{:S(2)}) collective-permute-start(bf16[96,384]{1,0:T(8,128)(2,1)S(1)} %get-tuple-element.122.refs_4_), channel_id=1, source_target_pairs={{0,24},{4,28},{8,0},{12,4},{16,8},{20,12},{24,16},{28,20},{1,25},{... | collective-permute-start | bytes 221192 | tf_op jit(solution)/shard_map/ppermute | solution.py:124
  11.6 1.1 collective-permute-start.4
  14.2 1.7 copy-done.1
  17.9 3.3 %shard_map.451 = (f32[768,768]{1,0:T(8,128)S(1)}, bf16[768,768]{1,0:T(8,128)(2,1)S(1)}, f32[768,768]{1,0:T(8,128)S(1)}, bf16[768,768]{1,0:T(8,128)(2,1)S(1)}) custom-call(s32[1,13]{1,0:T(1,128)S(1)} %copy-done.30, s32[1,7]{1,0:T(1,128)S(1)} %copy-done.28, bf16[96,384]{1,0:T(8,128)(2,1)S(1)} %get-tuple-element.119.refs_2_.refs_4_, ...), custom_call_target="tpu_custom_call" | custom-call | tf_op jit(solution)/shard_map/pallas_call | solution.py:59
  22.4 1.6 collective-permute-start.6
  24.5 2.4 collective-permute-start.10
  26.8 1.5 collective-permute-start.8
  29.1 4.1 %collective-permute-done.10.refs_3_ = bf16[96,768]{1,0:T(8,128)(2,1)S(1)} collective-permute-done((bf16[96,768]{1,0:T(8,128)(2,1)S(1)}, bf16[96,768]{1,0:T(8,128)(2,1)S(1)}, u32[]{:S(2)}, u32[]{:S(2)}) %collective-permute-start.10) | collective-permute-done | bytes 147488 | tf_op jit(solution)/shard_map/ppermute | solution.py:124
  33.1 1.3 collective-permute-start.11
  34.4 9.6 %collective-permute-start.12 = (bf16[96,768]{1,0:T(8,128)(2,1)S(1)}, bf16[96,768]{1,0:T(8,128)(2,1)S(1)}, u32[]{:S(2)}, u32[]{:S(2)}) collective-permute-start(bf16[96,768]{1,0:T(8,128)(2,1)S(1)} %get-tuple-element.127.refs_4_), channel_id=1, source_target_pairs={{0,16},{4,20},{8,24},{12,28},{16,0},{20,4},{24,8},{28,12},{1,17},{... | collective-permute-start | bytes 442376 | tf_op jit(solution)/shard_map/ppermute | solution.py:124
  44.1 2.2 collective-permute-start.13
  46.6 6.2 %shard_map.457 = (bf16[768,192]{1,0:T(8,128)(2,1)S(1)}, bf16[768,576]{1,0:T(8,128)(2,1)S(1)}, f32[768,128]{1,0:T(8,128)S(1)}) custom-call(s32[1,13]{1,0:T(1,128)S(1)} %copy-done.30, bf16[768,192]{1,0:T(8,128)(2,1)S(1)} %get-tuple-element.123.refs_1_.refs_7_.refs_6_.refs_9_, bf16[768,768]{1,0:T(8,128)(2,1)S(1)} %get-tuple-element.124.refs_2_.refs_1_, ...), custom_call_target="tpu_custom_call" | custom-call | tf_op jit(solution)/shard_map/pallas_call | solution.py:59
  53.0 1.6 collective-permute-start.21
  55.1 1.5 collective-permute-start.14
  57.2 5.8 %collective-permute-done.14.refs_2_.refs_9_.refs_8_ = bf16[768,192]{1,0:T(8,128)(2,1)S(1)} collective-permute-done((bf16[768,192]{1,0:T(8,128)(2,1)S(1)}, bf16[768,192]{1,0:T(8,128)(2,1)S(1)}, u32[]{:S(2)}, u32[]{:S(2)}) %collective-permute-start.14) | collective-permute-done | bytes 294944 | tf_op jit(solution)/shard_map/ppermute | solution.py:116
  63.0 4.2 %collective-permute-done.15.refs_2_.refs_5_ = bf16[768,192]{1,0:T(8,128)(2,1)S(1)} collective-permute-done((bf16[768,192]{1,0:T(8,128)(2,1)S(1)}, bf16[768,192]{1,0:T(8,128)(2,1)S(1)}, u32[]{:S(2)}, u32[]{:S(2)}) %collective-permute-start.15) | collective-permute-done | bytes 294944 | tf_op jit(solution)/shard_map/ppermute | solution.py:116
  67.9 4.3 %shard_map.460 = (bf16[768,192]{1,0:T(8,128)(2,1)S(1)}, bf16[768,576]{1,0:T(8,128)(2,1)S(1)}, f32[768,128]{1,0:T(8,128)S(1)}) custom-call(s32[1,7]{1,0:T(1,128)S(1)} %copy-done.28, bf16[384,768]{1,0:T(8,128)(2,1)S(1)} %shard_map.459.refs_1_.refs_0_, bf16[768,192]{1,0:T(8,128)(2,1)S(1)} %collective-permute-done.14.refs_2_.refs_9_.refs_8_, ...), custom_call_target="tpu_custom_call" | custom-call | tf_op jit(solution)/shard_map/pallas_call | solution.py:59
  73.1 1.0 collective-permute-done.20.refs_1_
  74.8 9.5 %shard_map.463 = (f32[768,768]{1,0:T(8,128)S(1)}, bf16[768,768]{1,0:T(8,128)(2,1)S(1)}, bf16[768,768]{1,0:T(8,128)(2,1)S(1)}, bf16[768,768]{1,0:T(8,128)(2,1)S(1...) custom-call(s32[1,13]{1,0:T(1,128)S(1)} %copy-done.30, ...), custom_call_target="tpu_custom_call" | custom-call | tf_op jit(solution)/shard_map/pallas_call | solution.py:59
  84.8 1.5 collective-permute-start.24
  86.4 9.6 %collective-permute-done.24.refs_4_ = bf16[768,192]{1,0:T(8,128)(2,1)S(1)} collective-permute-done((bf16[768,192]{1,0:T(8,128)(2,1)S(1)}, bf16[768,192]{1,0:T(8,128)(2,1)S(1)}, u32[]{:S(2)}, u32[]{:S(2)}) %collective-permute-start.24) | collective-permute-done | bytes 294944 | tf_op jit(solution)/shard_map/ppermute | solution.py:116
  96.0 1.6 collective-permute-done.25.refs_5_
  97.7 9.0 %shard_map.465 = (f32[768,768]{1,0:T(8,128)S(1)}, bf16[768,768]{1,0:T(8,128)(2,1)S(1)}, bf16[768,768]{1,0:T(8,128)(2,1)S(1)}, bf16[768,768]{1,0:T(8,128)(2,1)S(1...) custom-call(s32[1,7]{1,0:T(1,128)S(1)} %copy-done.28, ...), custom_call_target="tpu_custom_call" | custom-call | tf_op jit(solution)/shard_map/pallas_call | solution.py:59
  106.8 1.5 collective-permute-start.27
  108.8 5.1 %shard_map.467 = (bf16[384,1536]{1,0:T(8,128)(2,1)S(1)}, bf16[384,1536]{1,0:T(8,128)(2,1)S(1)}) custom-call(bf16[384,768]{1,0:T(8,128)(2,1)S(1)} %shard_map.466.refs_0_, bf16[768,768]{1,0:T(8,128)(2,1)S(1)} %get-tuple-element.139.refs_1_, bf16[768,768]{1,0:T(8,128)(2,1)S(1)} %get-tuple-element.140.refs_2_, bf16[768,768]{1,0:T(8,128)(2,1)S(1)} %get-tuple-element.141.refs_3_, ...), custom_call_target="tpu_custom_call" | custom-call | tf_op jit(solution)/shard_map/pallas_call | solution.py:59
  114.0 1.1 shard_map.468
  115.1 1.0 copy-done.12
  116.1 1.1 shard_map.469
  117.2 5.2 %collective-permute-done.27.refs_2_ = bf16[384,768]{1,0:T(8,128)(2,1)S(1)} collective-permute-done((bf16[384,768]{1,0:T(8,128)(2,1)S(1)}, bf16[384,768]{1,0:T(8,128)(2,1)S(1)}, u32[]{:S(2)}, u32[]{:S(2)}) %collective-permute-start.27) | collective-permute-done | bytes 589856 | tf_op jit(solution)/shard_map/ppermute | solution.py:116
  122.7 1.6 collective-permute-start.30
  124.7 13.9 %shard_map.471 = (f32[768,768]{1,0:T(8,128)S(1)}, bf16[768,768]{1,0:T(8,128)(2,1)S(1)}, bf16[768,576]{1,0:T(8,128)(2,1)S(1)}, bf16[384,768]{1,0:T(8,128)(2,1)S(1...) custom-call(s32[1,13]{1,0:T(1,128)S(1)} %copy-done.30, ...), custom_call_target="tpu_custom_call" | custom-call | tf_op jit(solution)/shard_map/pallas_call | solution.py:59
  139.4 1.5 collective-permute-start.33
  142.2 10.0 %shard_map.474 = (f32[768,768]{1,0:T(8,128)S(1)}, bf16[768,768]{1,0:T(8,128)(2,1)S(1)}, bf16[768,576]{1,0:T(8,128)(2,1)S(1)}, bf16[384,768]{1,0:T(8,128)(2,1)S(1...) custom-call(s32[1,7]{1,0:T(1,128)S(1)} %copy-done.29, ...), custom_call_target="tpu_custom_call" | custom-call | tf_op jit(solution)/shard_map/pallas_call | solution.py:59
  152.7 1.5 collective-permute-start.34
  154.4 12.9 %collective-permute-done.33.refs_2_ = bf16[384,1536]{1,0:T(8,128)(2,1)S(1)} collective-permute-done((bf16[384,1536]{1,0:T(8,128)(2,1)S(1)}, bf16[384,1536]{1,0:T(8,128)(2,1)S(1)}, u32[]{:S(2)}, u32[]{:S(2)}) %collective-permute-start.33) | collective-permute-done | bytes 1179680 | tf_op jit(solution)/shard_map/ppermute | solution.py:116
  167.6 3.4 %shard_map.477 = (bf16[384,768]{1,0:T(8,128)(2,1)S(1)}, bf16[384,768]{1,0:T(8,128)(2,1)S(1)}) custom-call(f32[96,1536]{1,0:T(8,128)S(1)} %get-tuple-element.159.refs_0_.refs_4_, bf16[768,768]{1,0:T(8,128)(2,1)S(1)} %get-tuple-element.124.refs_2_.refs_1_, bf16[768,768]{1,0:T(8,128)(2,1)S(1)} %get-tuple-element.120.refs_0_.refs_3_.refs_2_, ...), custom_call_target="tpu_custom_call" | custom-call | tf_op jit(solution)/shard_map/pallas_call | solution.py:59
  171.0 1.6 collective-permute-start.35
  172.6 1.5 collective-permute-start.43
  174.9 10.7 %collective-permute-done.35.refs_2_ = bf16[384,768]{1,0:T(8,128)(2,1)S(1)} collective-permute-done((bf16[384,768]{1,0:T(8,128)(2,1)S(1)}, bf16[384,768]{1,0:T(8,128)(2,1)S(1)}, u32[]{:S(2)}, u32[]{:S(2)}) %collective-permute-start.35) | collective-permute-done | bytes 589856 | tf_op jit(solution)/shard_map/ppermute | solution.py:116
  185.9 1.6 collective-permute-start.49
  188.2 3.2 %collective-permute-start.40 = (bf16[96,1536]{1,0:T(8,128)(2,1)S(1)}, bf16[96,1536]{1,0:T(8,128)(2,1)S(1)}, u32[]{:S(2)}, u32[]{:S(2)}) collective-permute-start(bf16[96,1536]{1,0:T(8,128)(2,1)S(1)} %get-tuple-element.171), channel_id=1, source_target_pairs={{0,16},{4,20},{8,24},{12,28},{16,0},{20,4},{24,8},{28,12},{1,17},{... | collective-permute-start | bytes 884744 | tf_op jit(solution)/shard_map/ppermute | solution.py:397
  191.5 9.8 %collective-permute-done.46.refs_1_ = bf16[384,768]{1,0:T(8,128)(2,1)S(1)} collective-permute-done((bf16[384,768]{1,0:T(8,128)(2,1)S(1)}, bf16[384,768]{1,0:T(8,128)(2,1)S(1)}, u32[]{:S(2)}, u32[]{:S(2)}) %collective-permute-start.46) | collective-permute-done | bytes 589856 | tf_op jit(solution)/shard_map/ppermute | solution.py:116
  201.5 12.1 %collective-permute-done.49.refs_1_ = bf16[384,768]{1,0:T(8,128)(2,1)S(1)} collective-permute-done((bf16[384,768]{1,0:T(8,128)(2,1)S(1)}, bf16[384,768]{1,0:T(8,128)(2,1)S(1)}, u32[]{:S(2)}, u32[]{:S(2)}) %collective-permute-start.49) | collective-permute-done | bytes 589856 | tf_op jit(solution)/shard_map/ppermute | solution.py:116
  214.3 1.9 collective-permute-start.41
  216.2 7.1 %collective-permute-done.41.refs_7_ = bf16[96,1536]{1,0:T(8,128)(2,1)S(1)} collective-permute-done((bf16[96,1536]{1,0:T(8,128)(2,1)S(1)}, bf16[96,1536]{1,0:T(8,128)(2,1)S(1)}, u32[]{:S(2)}, u32[]{:S(2)}) %collective-permute-start.41) | collective-permute-done | bytes 294944 | tf_op jit(solution)/shard_map/ppermute | solution.py:397
  223.3 2.7 collective-permute-start.36
  226.0 1.6 collective-permute-start.37
  227.6 2.5 collective-permute-start.38
  230.1 3.8 %shard_map.480 = (f32[2,768,768]{2,1,0:T(8,128)}, f32[2,768]{1,0:T(2,128)S(1)}) custom-call(f32[96,768]{1,0:T(8,128)S(1)} %get-tuple-element.166.refs_0_, bf16[384,768]{1,0:T(8,128)(2,1)S(1)} %shard_map.478.refs_0_.refs_1_, bf16[384,768]{1,0:T(8,128)(2,1)S(1)} %collective-permute-done.42.refs_2_, f32[768,768]{1,0:T(8,128)S(1)} %get-tuple-element.130.refs_11_.refs_3_, ...), custom_call_target="tpu_custom_call" | custom-call | tf_op jit(solution)/shard_map/pallas_call | solution.py:521
  233.9 3.6 %shard_map.482 = (f32[2,768,768]{2,1,0:T(8,128)}, f32[2,768]{1,0:T(2,128)S(1)}) custom-call(f32[2,768]{1,0:T(2,128)S(1)} %get-tuple-element.174.refs_0_.refs_8_, bf16[384,768]{1,0:T(8,128)(2,1)S(1)} %shard_map.481.refs_1_, bf16[384,768]{1,0:T(8,128)(2,1)S(1)} %collective-permute-done.44.refs_2_, ...), custom_call_target="tpu_custom_call", output_to_operand_aliasing={{0}: (6, {})} | custom-call | tf_op jit(solution)/shard_map/pallas_call | solution.py:521
  238.5 3.6 %collective-permute-done.51 = f32[16,768]{1,0:T(8,128)S(1)} collective-permute-done((f32[16,768]{1,0:T(8,128)S(1)}, f32[16,768]{1,0:T(8,128)S(1)}, u32[]{:S(2)}, u32[]{:S(2)}) %collective-permute-start.51) | collective-permute-done | bytes 49184 | tf_op jit(solution)/shard_map/ppermute | solution.py:116
  242.1 2.9 %collective-permute-start.52 = (f32[16,768]{1,0:T(8,128)S(1)}, f32[16,768]{1,0:T(8,128)S(1)}, u32[]{:S(2)}, u32[]{:S(2)}) collective-permute-start(f32[16,768]{1,0:T(8,128)S(1)} %add.25), channel_id=1, source_target_pairs={{0,8},{4,12},{8,0},{12,4},{16,24},{20,28},{24,16},{28,20},{1,9},{5... | collective-permute-start | bytes 147464 | tf_op jit(solution)/shard_map/ppermute | solution.py:116
  245.0 2.1 collective-permute-done.52
  247.1 2.8 %collective-permute-start.53 = (f32[16,768]{1,0:T(8,128)S(1)}, f32[16,768]{1,0:T(8,128)S(1)}, u32[]{:S(2)}, u32[]{:S(2)}) collective-permute-start(f32[16,768]{1,0:T(8,128)S(1)} %add.26), channel_id=1, source_target_pairs={{0,16},{4,20},{8,24},{12,28},{16,0},{20,4},{24,8},{28,12},{1,17},{... | collective-permute-start | bytes 147464 | tf_op jit(solution)/shard_map/ppermute | solution.py:116
  250.1 3.7 %shard_map.488 = (bf16[2,768,768]{2,1,0:T(8,128)(2,1)}, f32[8,128]{1,0:T(8,128)S(1)}) custom-call(s32[1,13]{1,0:T(1,128)S(1)} %copy-done.31, s32[1,7]{1,0:T(1,128)S(1)} %copy-done.29, f32[16,768]{1,0:T(8,128)S(1)} %get-tuple-element.182.refs_2_, bf16[384,768]{1,0:T(8,128)(2,1)S(1)} %shard_map.485.refs_3_, ...), custom_call_target="tpu_custom_call" | custom-call | tf_op jit(solution)/shard_map/pallas_call | solution.py:59
  254.6 2.8 %collective-permute-done.56 = f32[8,128]{1,0:T(8,128)S(1)} collective-permute-done((f32[8,128]{1,0:T(8,128)S(1)}, f32[8,128]{1,0:T(8,128)S(1)}, u32[]{:S(2)}, u32[]{:S(2)}) %collective-permute-start.56) | collective-permute-done | bytes 4128 | tf_op jit(solution)/shard_map/ppermute | solution.py:116
  257.5 2.5 collective-permute-start.57
  260.0 1.5 collective-permute-start.55
  261.7 1.9 collective-permute-done.55.moved_ref
  263.8 4.1 %shard_map.490 = (f32[3,96,192]{2,1,0:T(8,128)}, f32[3,96,192]{2,1,0:T(8,128)}, f32[3,96,192]{2,1,0:T(8,128)}, f32[192,96]{1,0:T(8,128)}, f32[192,96]{1,0:T(8,12...) custom-call(f32[8,128]{1,0:T(8,128)S(1)} %add.28.partial_ref, ...), custom_call_target="tpu_custom_call" | custom-call | flops 10000000 | bytes 10000000 | tf_op jit(solution)/shard_map/pallas_call | solution.py:645
  (192 shorter events, 22.7 us)
Async XLA Ops:
  2.7 10.1 %collective-permute-start = (bf16[96,384]{1,0:T(8,128)(2,1)S(1)}, bf16[96,384]{1,0:T(8,128)(2,1)S(1)}, u32[]{:S(2)}, u32[]{:S(2)}) collective-permute-start(bf16[96,384]{1,0:T(8,128)(2,1)S(1)} %get-tuple-element.119.refs_2_.refs_4_), channel_id=1, source_target_pairs={{0,24},{4,28},{8,0},{12,4},{16,8},{20,12},{24,16},{28,20},{1,25},{... | collective-permute-start | bytes 221192 | tf_op jit(solution)/shard_map/ppermute | solution.py:124
  7.8 13.4 %collective-permute-start.1 = (bf16[96,384]{1,0:T(8,128)(2,1)S(1)}, bf16[96,384]{1,0:T(8,128)(2,1)S(1)}, u32[]{:S(2)}, u32[]{:S(2)}) collective-permute-start(bf16[96,384]{1,0:T(8,128)(2,1)S(1)} %get-tuple-element.119.refs_2_.refs_4_), channel_id=1, source_target_pairs={{0,16},{4,20},{8,24},{12,28},{16,0},{20,4},{24,8},{28,12},{1,17},{... | collective-permute-start | bytes 221192 | tf_op jit(solution)/shard_map/ppermute | solution.py:124
  7.8 13.4 %collective-permute-start.2 = (bf16[96,384]{1,0:T(8,128)(2,1)S(1)}, bf16[96,384]{1,0:T(8,128)(2,1)S(1)}, u32[]{:S(2)}, u32[]{:S(2)}) collective-permute-start(bf16[96,384]{1,0:T(8,128)(2,1)S(1)} %get-tuple-element.119.refs_2_.refs_4_), channel_id=1, source_target_pairs={{0,8},{4,12},{8,16},{12,20},{16,24},{20,28},{24,0},{28,4},{1,9},{5... | collective-permute-start | bytes 221192 | tf_op jit(solution)/shard_map/ppermute | solution.py:124
  8.8 13.5 %collective-permute-start.3 = (bf16[96,384]{1,0:T(8,128)(2,1)S(1)}, bf16[96,384]{1,0:T(8,128)(2,1)S(1)}, u32[]{:S(2)}, u32[]{:S(2)}) collective-permute-start(bf16[96,384]{1,0:T(8,128)(2,1)S(1)} %get-tuple-element.122.refs_4_), channel_id=1, source_target_pairs={{0,24},{4,28},{8,0},{12,4},{16,8},{20,12},{24,16},{28,20},{1,25},{... | collective-permute-start | bytes 221192 | tf_op jit(solution)/shard_map/ppermute | solution.py:124
  11.6 10.7 %collective-permute-start.4 = (bf16[96,384]{1,0:T(8,128)(2,1)S(1)}, bf16[96,384]{1,0:T(8,128)(2,1)S(1)}, u32[]{:S(2)}, u32[]{:S(2)}) collective-permute-start(bf16[96,384]{1,0:T(8,128)(2,1)S(1)} %get-tuple-element.122.refs_4_), channel_id=1, source_target_pairs={{0,16},{4,20},{8,24},{12,28},{16,0},{20,4},{24,8},{28,12},{1,17},{... | collective-permute-start | bytes 221192 | tf_op jit(solution)/shard_map/ppermute | solution.py:124
  12.8 9.6 %collective-permute-start.5 = (bf16[96,384]{1,0:T(8,128)(2,1)S(1)}, bf16[96,384]{1,0:T(8,128)(2,1)S(1)}, u32[]{:S(2)}, u32[]{:S(2)}) collective-permute-start(bf16[96,384]{1,0:T(8,128)(2,1)S(1)} %get-tuple-element.122.refs_4_), channel_id=1, source_target_pairs={{0,8},{4,12},{8,16},{12,20},{16,24},{20,28},{24,0},{28,4},{1,9},{5... | collective-permute-start | bytes 221192 | tf_op jit(solution)/shard_map/ppermute | solution.py:124
  21.3 25.0 %copy-start.32 = (f32[2,192]{1,0:T(2,128)S(1)}, f32[2,192]{1,0:T(2,128)}, u32[]{:S(2)}) copy-start(f32[2,192]{1,0:T(2,128)} %refs_15_.3) | copy-start | bytes 4612
  22.4 12.1 %collective-permute-start.6 = (bf16[384,384]{1,0:T(8,128)(2,1)S(1)}, bf16[384,384]{1,0:T(8,128)(2,1)S(1)}, u32[]{:S(2)}, u32[]{:S(2)}) collective-permute-start(bf16[384,384]{1,0:T(8,128)(2,1)S(1)} %shard_map.454.refs_0_), channel_id=1, source_target_pairs={{0,4},{4,0},{8,12},{12,8},{16,20},{20,16},{24,28},{28,24},{1,5},{5... | collective-permute-start | bytes 884744 | tf_op jit(solution)/shard_map/ppermute | solution.py:116
  23.9 20.1 %collective-permute-start.7 = (bf16[384,384]{1,0:T(8,128)(2,1)S(1)}, bf16[384,384]{1,0:T(8,128)(2,1)S(1)}, u32[]{:S(2)}, u32[]{:S(2)}) collective-permute-start(bf16[384,384]{1,0:T(8,128)(2,1)S(1)} %shard_map.452.refs_0_), channel_id=1, source_target_pairs={{0,4},{4,0},{8,12},{12,8},{16,20},{20,16},{24,28},{28,24},{1,5},{5... | collective-permute-start | bytes 884744 | tf_op jit(solution)/shard_map/ppermute | solution.py:116
  24.5 8.7 %collective-permute-start.10 = (bf16[96,768]{1,0:T(8,128)(2,1)S(1)}, bf16[96,768]{1,0:T(8,128)(2,1)S(1)}, u32[]{:S(2)}, u32[]{:S(2)}) collective-permute-start(bf16[96,768]{1,0:T(8,128)(2,1)S(1)} %get-tuple-element.121.refs_0_.refs_4_), channel_id=1, source_target_pairs={{0,8},{4,12},{8,16},{12,20},{16,24},{20,28},{24,0},{28,4},{1,9},{5... | collective-permute-start | bytes 442376 | tf_op jit(solution)/shard_map/ppermute | solution.py:124
  26.8 26.1 %collective-permute-start.8 = (bf16[96,768]{1,0:T(8,128)(2,1)S(1)}, bf16[96,768]{1,0:T(8,128)(2,1)S(1)}, u32[]{:S(2)}, u32[]{:S(2)}) collective-permute-start(bf16[96,768]{1,0:T(8,128)(2,1)S(1)} %get-tuple-element.121.refs_0_.refs_4_), channel_id=1, source_target_pairs={{0,24},{4,28},{8,0},{12,4},{16,8},{20,12},{24,16},{28,20},{1,25},{... | collective-permute-start | bytes 442376 | tf_op jit(solution)/shard_map/ppermute | solution.py:124
  28.3 24.6 %collective-permute-start.9 = (bf16[96,768]{1,0:T(8,128)(2,1)S(1)}, bf16[96,768]{1,0:T(8,128)(2,1)S(1)}, u32[]{:S(2)}, u32[]{:S(2)}) collective-permute-start(bf16[96,768]{1,0:T(8,128)(2,1)S(1)} %get-tuple-element.121.refs_0_.refs_4_), channel_id=1, source_target_pairs={{0,16},{4,20},{8,24},{12,28},{16,0},{20,4},{24,8},{28,12},{1,17},{... | collective-permute-start | bytes 442376 | tf_op jit(solution)/shard_map/ppermute | solution.py:124
  33.1 19.8 %collective-permute-start.11 = (bf16[96,768]{1,0:T(8,128)(2,1)S(1)}, bf16[96,768]{1,0:T(8,128)(2,1)S(1)}, u32[]{:S(2)}, u32[]{:S(2)}) collective-permute-start(bf16[96,768]{1,0:T(8,128)(2,1)S(1)} %get-tuple-element.127.refs_4_), channel_id=1, source_target_pairs={{0,24},{4,28},{8,0},{12,4},{16,8},{20,12},{24,16},{28,20},{1,25},{... | collective-permute-start | bytes 442376 | tf_op jit(solution)/shard_map/ppermute | solution.py:124
  34.4 18.6 %collective-permute-start.12 = (bf16[96,768]{1,0:T(8,128)(2,1)S(1)}, bf16[96,768]{1,0:T(8,128)(2,1)S(1)}, u32[]{:S(2)}, u32[]{:S(2)}) collective-permute-start(bf16[96,768]{1,0:T(8,128)(2,1)S(1)} %get-tuple-element.127.refs_4_), channel_id=1, source_target_pairs={{0,16},{4,20},{8,24},{12,28},{16,0},{20,4},{24,8},{28,12},{1,17},{... | collective-permute-start | bytes 442376 | tf_op jit(solution)/shard_map/ppermute | solution.py:124
  44.1 8.9 %collective-permute-start.13 = (bf16[96,768]{1,0:T(8,128)(2,1)S(1)}, bf16[96,768]{1,0:T(8,128)(2,1)S(1)}, u32[]{:S(2)}, u32[]{:S(2)}) collective-permute-start(bf16[96,768]{1,0:T(8,128)(2,1)S(1)} %get-tuple-element.127.refs_4_), channel_id=1, source_target_pairs={{0,8},{4,12},{8,16},{12,20},{16,24},{20,28},{24,0},{28,4},{1,9},{5... | collective-permute-start | bytes 442376 | tf_op jit(solution)/shard_map/ppermute | solution.py:124
  52.9 14.9 %copy-start.35 = (f32[768]{0:T(1024)S(1)}, f32[768]{0:T(1024)}, u32[]{:S(2)}) copy-start(f32[768]{0:T(1024)} %param.51) | copy-start | bytes 9220
  53.0 14.8 %collective-permute-start.21 = (bf16[384,768]{1,0:T(8,128)(2,1)S(1)}, bf16[384,768]{1,0:T(8,128)(2,1)S(1)}, u32[]{:S(2)}, u32[]{:S(2)}) collective-permute-start(bf16[384,768]{1,0:T(8,128)(2,1)S(1)} %shard_map.459.refs_1_.refs_0_), channel_id=1, source_target_pairs={{0,4},{4,0},{8,12},{12,8},{16,20},{20,16},{24,28},{28,24},{1,5},{5... | collective-permute-start | bytes 1769480 | tf_op jit(solution)/shard_map/ppermute | solution.py:116
  54.6 19.6 %collective-permute-start.20 = (bf16[384,768]{1,0:T(8,128)(2,1)S(1)}, bf16[384,768]{1,0:T(8,128)(2,1)S(1)}, u32[]{:S(2)}, u32[]{:S(2)}) collective-permute-start(bf16[384,768]{1,0:T(8,128)(2,1)S(1)} %shard_map.458.refs_0_), channel_id=1, source_target_pairs={{0,4},{4,0},{8,12},{12,8},{16,20},{20,16},{24,28},{28,24},{1,5},{5... | collective-permute-start | bytes 1769480 | tf_op jit(solution)/shard_map/ppermute | solution.py:116
  55.1 7.9 %collective-permute-start.14 = (bf16[768,192]{1,0:T(8,128)(2,1)S(1)}, bf16[768,192]{1,0:T(8,128)(2,1)S(1)}, u32[]{:S(2)}, u32[]{:S(2)}) collective-permute-start(bf16[768,192]{1,0:T(8,128)(2,1)S(1)} %get-tuple-element.123.refs_1_.refs_7_.refs_6_.refs_9_), channel_id=1, source_target_pairs={{0,2},{1,3},{2,0},{3,1},{4,6},{5,7},{6,4},{7,5},{8,10},{9,11},{10,... | collective-permute-start | bytes 884744 | tf_op jit(solution)/shard_map/ppermute | solution.py:116
  56.6 10.6 %collective-permute-start.15 = (bf16[768,192]{1,0:T(8,128)(2,1)S(1)}, bf16[768,192]{1,0:T(8,128)(2,1)S(1)}, u32[]{:S(2)}, u32[]{:S(2)}) collective-permute-start(bf16[768,192]{1,0:T(8,128)(2,1)S(1)} %get-tuple-element.129.refs_3_.refs_7_), channel_id=1, source_target_pairs={{0,2},{1,3},{2,0},{3,1},{4,6},{5,7},{6,4},{7,5},{8,10},{9,11},{10,... | collective-permute-start | bytes 884744 | tf_op jit(solution)/shard_map/ppermute | solution.py:116
  57.2 17.1 %collective-permute-start.16 = (bf16[768,192]{1,0:T(8,128)(2,1)S(1)}, bf16[768,192]{1,0:T(8,128)(2,1)S(1)}, u32[]{:S(2)}, u32[]{:S(2)}) collective-permute-start(bf16[768,192]{1,0:T(8,128)(2,1)S(1)} %get-tuple-element.129.refs_3_.refs_7_), channel_id=1, source_target_pairs={{0,1},{1,0},{2,3},{3,2},{4,5},{5,4},{6,7},{7,6},{8,9},{9,8},{10,11... | collective-permute-start | bytes 884744 | tf_op jit(solution)/shard_map/ppermute | solution.py:116
  63.0 11.3 %collective-permute-start.18 = (bf16[768,192]{1,0:T(8,128)(2,1)S(1)}, bf16[768,192]{1,0:T(8,128)(2,1)S(1)}, u32[]{:S(2)}, u32[]{:S(2)}) collective-permute-start(bf16[768,192]{1,0:T(8,128)(2,1)S(1)} %get-tuple-element.123.refs_1_.refs_7_.refs_6_.refs_9_), channel_id=1, source_target_pairs={{0,1},{1,0},{2,3},{3,2},{4,5},{5,4},{6,7},{7,6},{8,9},{9,8},{10,11... | collective-permute-start | bytes 884744 | tf_op jit(solution)/shard_map/ppermute | solution.py:116
  67.2 7.1 %collective-permute-start.17 = (bf16[768,192]{1,0:T(8,128)(2,1)S(1)}, bf16[768,192]{1,0:T(8,128)(2,1)S(1)}, u32[]{:S(2)}, u32[]{:S(2)}) collective-permute-start(bf16[768,192]{1,0:T(8,128)(2,1)S(1)} %collective-permute-done.15.refs_2_.refs_5_), channel_id=1, source_target_pairs={{0,1},{1,0},{2,3},{3,2},{4,5},{5,4},{6,7},{7,6},{8,9},{9,8},{10,11... | collective-permute-start | bytes 884744 | tf_op jit(solution)/shard_map/ppermute | solution.py:116
  67.9 6.5 %collective-permute-start.19 = (bf16[768,192]{1,0:T(8,128)(2,1)S(1)}, bf16[768,192]{1,0:T(8,128)(2,1)S(1)}, u32[]{:S(2)}, u32[]{:S(2)}) collective-permute-start(bf16[768,192]{1,0:T(8,128)(2,1)S(1)} %collective-permute-done.14.refs_2_.refs_9_.refs_8_), channel_id=1, source_target_pairs={{0,1},{1,0},{2,3},{3,2},{4,5},{5,4},{6,7},{7,6},{8,9},{9,8},{10,11... | collective-permute-start | bytes 884744 | tf_op jit(solution)/shard_map/ppermute | solution.py:116
  84.3 11.7 %collective-permute-start.22 = (bf16[384,768]{1,0:T(8,128)(2,1)S(1)}, bf16[384,768]{1,0:T(8,128)(2,1)S(1)}, u32[]{:S(2)}, u32[]{:S(2)}) collective-permute-start(bf16[384,768]{1,0:T(8,128)(2,1)S(1)} %get-tuple-element.133), channel_id=1, source_target_pairs={{0,1},{1,0},{2,3},{3,2},{4,5},{5,4},{6,7},{7,6},{8,9},{9,8},{10,11... | collective-permute-start | bytes 1769480 | tf_op jit(solution)/shard_map/ppermute | solution.py:116
  84.8 11.1 %collective-permute-start.24 = (bf16[768,192]{1,0:T(8,128)(2,1)S(1)}, bf16[768,192]{1,0:T(8,128)(2,1)S(1)}, u32[]{:S(2)}, u32[]{:S(2)}) collective-permute-start(bf16[768,192]{1,0:T(8,128)(2,1)S(1)} %get-tuple-element.134.refs_2_.refs_8_), channel_id=1, source_target_pairs={{0,2},{1,3},{2,0},{3,1},{4,6},{5,7},{6,4},{7,5},{8,10},{9,11},{10,... | collective-permute-start | bytes 884744 | tf_op jit(solution)/shard_map/ppermute | solution.py:116
  86.3 9.7 %collective-permute-start.23 = (bf16[768,192]{1,0:T(8,128)(2,1)S(1)}, bf16[768,192]{1,0:T(8,128)(2,1)S(1)}, u32[]{:S(2)}, u32[]{:S(2)}) collective-permute-start(bf16[768,192]{1,0:T(8,128)(2,1)S(1)} %get-tuple-element.134.refs_2_.refs_8_), channel_id=1, source_target_pairs={{0,1},{1,0},{2,3},{3,2},{4,5},{5,4},{6,7},{7,6},{8,9},{9,8},{10,11... | collective-permute-start | bytes 884744 | tf_op jit(solution)/shard_map/ppermute | solution.py:116
  95.9 1.7 collective-permute-start.25
  106.6 2.1 collective-permute-start.26
  106.8 15.6 %collective-permute-start.27 = (bf16[384,768]{1,0:T(8,128)(2,1)S(1)}, bf16[384,768]{1,0:T(8,128)(2,1)S(1)}, u32[]{:S(2)}, u32[]{:S(2)}) collective-permute-start(bf16[384,768]{1,0:T(8,128)(2,1)S(1)} %shard_map.464.refs_1_), channel_id=1, source_target_pairs={{0,2},{1,3},{2,0},{3,1},{4,6},{5,7},{6,4},{7,5},{8,10},{9,11},{10,... | collective-permute-start | bytes 1769480 | tf_op jit(solution)/shard_map/ppermute | solution.py:116
  122.6 2.1 collective-permute-start.28
  122.7 16.0 %collective-permute-start.30 = (bf16[384,768]{1,0:T(8,128)(2,1)S(1)}, bf16[384,768]{1,0:T(8,128)(2,1)S(1)}, u32[]{:S(2)}, u32[]{:S(2)}) collective-permute-start(bf16[384,768]{1,0:T(8,128)(2,1)S(1)} %shard_map.466.refs_0_), channel_id=1, source_target_pairs={{0,2},{1,3},{2,0},{3,1},{4,6},{5,7},{6,4},{7,5},{8,10},{9,11},{10,... | collective-permute-start | bytes 1769480 | tf_op jit(solution)/shard_map/ppermute | solution.py:116
  138.6 2.3 collective-permute-start.29
  138.9 2.6 collective-permute-start.31
  139.4 28.0 %collective-permute-start.33 = (bf16[384,1536]{1,0:T(8,128)(2,1)S(1)}, bf16[384,1536]{1,0:T(8,128)(2,1)S(1)}, u32[]{:S(2)}, u32[]{:S(2)}) collective-permute-start(bf16[384,1536]{1,0:T(8,128)(2,1)S(1)} %get-tuple-element.147.refs_0_), channel_id=1, source_target_pairs={{0,4},{4,0},{8,12},{12,8},{16,20},{20,16},{24,28},{28,24},{1,5},{5... | collective-permute-start | bytes 3538952 | tf_op jit(solution)/shard_map/ppermute | solution.py:116
  152.1 2.1 collective-permute-start.32
  152.2 21.9 %collective-permute-start.45 = (bf16[384,768]{1,0:T(8,128)(2,1)S(1)}, bf16[384,768]{1,0:T(8,128)(2,1)S(1)}, u32[]{:S(2)}, u32[]{:S(2)}) collective-permute-start(bf16[384,768]{1,0:T(8,128)(2,1)S(1)} %get-tuple-element.148.refs_0_), channel_id=1, source_target_pairs={{0,1},{1,0},{2,3},{3,2},{4,5},{5,4},{6,7},{7,6},{8,9},{9,8},{10,11... | collective-permute-start | bytes 1769480 | tf_op jit(solution)/shard_map/ppermute | solution.py:116
  152.7 22.1 %collective-permute-start.34 = (bf16[384,768]{1,0:T(8,128)(2,1)S(1)}, bf16[384,768]{1,0:T(8,128)(2,1)S(1)}, u32[]{:S(2)}, u32[]{:S(2)}) collective-permute-start(bf16[384,768]{1,0:T(8,128)(2,1)S(1)} %shard_map.472.refs_1_), channel_id=1, source_target_pairs={{0,2},{1,3},{2,0},{3,1},{4,6},{5,7},{6,4},{7,5},{8,10},{9,11},{10,... | collective-permute-start | bytes 1769480 | tf_op jit(solution)/shard_map/ppermute | solution.py:116
  171.0 14.6 %collective-permute-start.35 = (bf16[384,768]{1,0:T(8,128)(2,1)S(1)}, bf16[384,768]{1,0:T(8,128)(2,1)S(1)}, u32[]{:S(2)}, u32[]{:S(2)}) collective-permute-start(bf16[384,768]{1,0:T(8,128)(2,1)S(1)} %get-tuple-element.164.refs_0_), channel_id=1, source_target_pairs={{0,4},{4,0},{8,12},{12,8},{16,20},{20,16},{24,28},{28,24},{1,5},{5... | collective-permute-start | bytes 1769480 | tf_op jit(solution)/shard_map/ppermute | solution.py:116
  172.6 13.2 %collective-permute-start.48 = (bf16[384,768]{1,0:T(8,128)(2,1)S(1)}, bf16[384,768]{1,0:T(8,128)(2,1)S(1)}, u32[]{:S(2)}, u32[]{:S(2)}) collective-permute-start(bf16[384,768]{1,0:T(8,128)(2,1)S(1)} %get-tuple-element.149.refs_0_), channel_id=1, source_target_pairs={{0,1},{1,0},{2,3},{3,2},{4,5},{5,4},{6,7},{7,6},{8,9},{9,8},{10,11... | collective-permute-start | bytes 1769480 | tf_op jit(solution)/shard_map/ppermute | solution.py:116
  172.6 18.8 %collective-permute-start.43 = (bf16[384,768]{1,0:T(8,128)(2,1)S(1)}, bf16[384,768]{1,0:T(8,128)(2,1)S(1)}, u32[]{:S(2)}, u32[]{:S(2)}) collective-permute-start(bf16[384,768]{1,0:T(8,128)(2,1)S(1)} %shard_map.475.refs_0_.refs_1_), channel_id=1, source_target_pairs={{0,2},{1,3},{2,0},{3,1},{4,6},{5,7},{6,4},{7,5},{8,10},{9,11},{10,... | collective-permute-start | bytes 1769480 | tf_op jit(solution)/shard_map/ppermute | solution.py:116
  174.2 27.1 %collective-permute-start.46 = (bf16[384,768]{1,0:T(8,128)(2,1)S(1)}, bf16[384,768]{1,0:T(8,128)(2,1)S(1)}, u32[]{:S(2)}, u32[]{:S(2)}) collective-permute-start(bf16[384,768]{1,0:T(8,128)(2,1)S(1)} %shard_map.484.refs_0_), channel_id=1, source_target_pairs={{0,2},{1,3},{2,0},{3,1},{4,6},{5,7},{6,4},{7,5},{8,10},{9,11},{10,... | collective-permute-start | bytes 1769480 | tf_op jit(solution)/shard_map/ppermute | solution.py:116
  185.9 27.7 %collective-permute-start.49 = (bf16[384,768]{1,0:T(8,128)(2,1)S(1)}, bf16[384,768]{1,0:T(8,128)(2,1)S(1)}, u32[]{:S(2)}, u32[]{:S(2)}) collective-permute-start(bf16[384,768]{1,0:T(8,128)(2,1)S(1)} %shard_map.486.refs_0_), channel_id=1, source_target_pairs={{0,2},{1,3},{2,0},{3,1},{4,6},{5,7},{6,4},{7,5},{8,10},{9,11},{10,... | collective-permute-start | bytes 1769480 | tf_op jit(solution)/shard_map/ppermute | solution.py:116
  187.5 26.3 %collective-permute-start.39 = (bf16[96,1536]{1,0:T(8,128)(2,1)S(1)}, bf16[96,1536]{1,0:T(8,128)(2,1)S(1)}, u32[]{:S(2)}, u32[]{:S(2)}) collective-permute-start(bf16[96,1536]{1,0:T(8,128)(2,1)S(1)} %get-tuple-element.170), channel_id=1, source_target_pairs={{0,8},{4,12},{8,16},{12,20},{16,24},{20,28},{24,0},{28,4},{1,9},{5... | collective-permute-start | bytes 884744 | tf_op jit(solution)/shard_map/ppermute | solution.py:397
  188.2 26.1 %collective-permute-start.40 = (bf16[96,1536]{1,0:T(8,128)(2,1)S(1)}, bf16[96,1536]{1,0:T(8,128)(2,1)S(1)}, u32[]{:S(2)}, u32[]{:S(2)}) collective-permute-start(bf16[96,1536]{1,0:T(8,128)(2,1)S(1)} %get-tuple-element.171), channel_id=1, source_target_pairs={{0,16},{4,20},{8,24},{12,28},{16,0},{20,4},{24,8},{28,12},{1,17},{... | collective-permute-start | bytes 884744 | tf_op jit(solution)/shard_map/ppermute | solution.py:397
  191.4 34.7 %collective-permute-start.42 = (bf16[384,768]{1,0:T(8,128)(2,1)S(1)}, bf16[384,768]{1,0:T(8,128)(2,1)S(1)}, u32[]{:S(2)}, u32[]{:S(2)}) collective-permute-start(bf16[384,768]{1,0:T(8,128)(2,1)S(1)} %shard_map.478.refs_0_.refs_1_), channel_id=1, source_target_pairs={{0,1},{1,0},{2,3},{3,2},{4,5},{5,4},{6,7},{7,6},{8,9},{9,8},{10,11... | collective-permute-start | bytes 1769480 | tf_op jit(solution)/shard_map/ppermute | solution.py:116
  201.4 26.2 %collective-permute-start.44 = (bf16[384,768]{1,0:T(8,128)(2,1)S(1)}, bf16[384,768]{1,0:T(8,128)(2,1)S(1)}, u32[]{:S(2)}, u32[]{:S(2)}) collective-permute-start(bf16[384,768]{1,0:T(8,128)(2,1)S(1)} %shard_map.481.refs_1_), channel_id=1, source_target_pairs={{0,1},{1,0},{2,3},{3,2},{4,5},{5,4},{6,7},{7,6},{8,9},{9,8},{10,11... | collective-permute-start | bytes 1769480 | tf_op jit(solution)/shard_map/ppermute | solution.py:116
  213.6 36.3 %collective-permute-start.47 = (bf16[384,768]{1,0:T(8,128)(2,1)S(1)}, bf16[384,768]{1,0:T(8,128)(2,1)S(1)}, u32[]{:S(2)}, u32[]{:S(2)}) collective-permute-start(bf16[384,768]{1,0:T(8,128)(2,1)S(1)} %shard_map.485.refs_3_), channel_id=1, source_target_pairs={{0,1},{1,0},{2,3},{3,2},{4,5},{5,4},{6,7},{7,6},{8,9},{9,8},{10,11... | collective-permute-start | bytes 1769480 | tf_op jit(solution)/shard_map/ppermute | solution.py:116
  213.8 36.2 %collective-permute-start.50 = (bf16[384,768]{1,0:T(8,128)(2,1)S(1)}, bf16[384,768]{1,0:T(8,128)(2,1)S(1)}, u32[]{:S(2)}, u32[]{:S(2)}) collective-permute-start(bf16[384,768]{1,0:T(8,128)(2,1)S(1)} %shard_map.487.refs_6_), channel_id=1, source_target_pairs={{0,1},{1,0},{2,3},{3,2},{4,5},{5,4},{6,7},{7,6},{8,9},{9,8},{10,11... | collective-permute-start | bytes 1769480 | tf_op jit(solution)/shard_map/ppermute | solution.py:116
  214.3 9.0 %collective-permute-start.41 = (bf16[96,1536]{1,0:T(8,128)(2,1)S(1)}, bf16[96,1536]{1,0:T(8,128)(2,1)S(1)}, u32[]{:S(2)}, u32[]{:S(2)}) collective-permute-start(bf16[96,1536]{1,0:T(8,128)(2,1)S(1)} %get-tuple-element.172), channel_id=1, source_target_pairs={{0,24},{4,28},{8,0},{12,4},{16,8},{20,12},{24,16},{28,20},{1,25},{... | collective-permute-start | bytes 884744 | tf_op jit(solution)/shard_map/ppermute | solution.py:397
  223.3 14.2 %collective-permute-start.36 = (bf16[96,768]{1,0:T(8,128)(2,1)S(1)}, bf16[96,768]{1,0:T(8,128)(2,1)S(1)}, u32[]{:S(2)}, u32[]{:S(2)}) collective-permute-start(bf16[96,768]{1,0:T(8,128)(2,1)S(1)} %get-tuple-element.167), channel_id=1, source_target_pairs={{0,8},{4,12},{8,16},{12,20},{16,24},{20,28},{24,0},{28,4},{1,9},{5... | collective-permute-start | bytes 442376 | tf_op jit(solution)/shard_map/ppermute | solution.py:397
  226.0 11.5 %collective-permute-start.37 = (bf16[96,768]{1,0:T(8,128)(2,1)S(1)}, bf16[96,768]{1,0:T(8,128)(2,1)S(1)}, u32[]{:S(2)}, u32[]{:S(2)}) collective-permute-start(bf16[96,768]{1,0:T(8,128)(2,1)S(1)} %get-tuple-element.168), channel_id=1, source_target_pairs={{0,16},{4,20},{8,24},{12,28},{16,0},{20,4},{24,8},{28,12},{1,17},{... | collective-permute-start | bytes 442376 | tf_op jit(solution)/shard_map/ppermute | solution.py:397
  227.6 9.9 %collective-permute-start.38 = (bf16[96,768]{1,0:T(8,128)(2,1)S(1)}, bf16[96,768]{1,0:T(8,128)(2,1)S(1)}, u32[]{:S(2)}, u32[]{:S(2)}) collective-permute-start(bf16[96,768]{1,0:T(8,128)(2,1)S(1)} %get-tuple-element.169), channel_id=1, source_target_pairs={{0,24},{4,28},{8,0},{12,4},{16,8},{20,12},{24,16},{28,20},{1,25},{... | collective-permute-start | bytes 442376 | tf_op jit(solution)/shard_map/ppermute | solution.py:397
  238.0 4.1 %collective-permute-start.51 = (f32[16,768]{1,0:T(8,128)S(1)}, f32[16,768]{1,0:T(8,128)S(1)}, u32[]{:S(2)}, u32[]{:S(2)}) collective-permute-start(f32[16,768]{1,0:T(8,128)S(1)} %get-tuple-element.182.refs_2_), channel_id=1, source_target_pairs={{0,4},{4,0},{8,12},{12,8},{16,20},{20,16},{24,28},{28,24},{1,5},{5... | collective-permute-start | bytes 147464 | tf_op jit(solution)/shard_map/ppermute | solution.py:116
  242.1 5.0 %collective-permute-start.52 = (f32[16,768]{1,0:T(8,128)S(1)}, f32[16,768]{1,0:T(8,128)S(1)}, u32[]{:S(2)}, u32[]{:S(2)}) collective-permute-start(f32[16,768]{1,0:T(8,128)S(1)} %add.25), channel_id=1, source_target_pairs={{0,8},{4,12},{8,0},{12,4},{16,24},{20,28},{24,16},{28,20},{1,9},{5... | collective-permute-start | bytes 147464 | tf_op jit(solution)/shard_map/ppermute | solution.py:116
  247.1 7.3 %collective-permute-start.53 = (f32[16,768]{1,0:T(8,128)S(1)}, f32[16,768]{1,0:T(8,128)S(1)}, u32[]{:S(2)}, u32[]{:S(2)}) collective-permute-start(f32[16,768]{1,0:T(8,128)S(1)} %add.26), channel_id=1, source_target_pairs={{0,16},{4,20},{8,24},{12,28},{16,0},{20,4},{24,8},{28,12},{1,17},{... | collective-permute-start | bytes 147464 | tf_op jit(solution)/shard_map/ppermute | solution.py:116
  250.0 13.7 %copy-start.9 = (f32[96,3,192]{2,0,1:T(8,128)S(1)}, f32[96,3,192]{2,0,1:T(8,128)}, u32[]{:S(2)}) copy-start(f32[96,3,192]{2,0,1:T(8,128)} %param.33) | copy-start | bytes 663556
  250.0 13.7 %copy-start.17 = (f32[192,96]{1,0:T(8,128)S(1)}, f32[192,96]{1,0:T(8,128)}, u32[]{:S(2)}) copy-start(f32[192,96]{1,0:T(8,128)} %refs_3_.3) | copy-start | bytes 221188
  250.0 13.7 %copy-start.18 = (f32[96,3,192]{2,0,1:T(8,128)S(1)}, f32[96,3,192]{2,0,1:T(8,128)}, u32[]{:S(2)}) copy-start(f32[96,3,192]{2,0,1:T(8,128)} %param.34) | copy-start | bytes 663556
  253.9 3.6 %collective-permute-start.56 = (f32[8,128]{1,0:T(8,128)S(1)}, f32[8,128]{1,0:T(8,128)S(1)}, u32[]{:S(2)}, u32[]{:S(2)}) collective-permute-start(f32[8,128]{1,0:T(8,128)S(1)} %get-tuple-element.191), channel_id=1, source_target_pairs={{0,4},{4,0},{8,12},{12,8},{16,20},{20,16},{24,28},{28,24},{1,5},{5... | collective-permute-start | bytes 12296 | tf_op jit(solution)/shard_map/ppermute | solution.py:116
  254.5 5.5 %collective-permute-start.54 = (f32[8,128]{1,0:T(8,128)S(1)}, f32[8,128]{1,0:T(8,128)S(1)}, u32[]{:S(2)}, u32[]{:S(2)}) collective-permute-start(f32[8,128]{1,0:T(8,128)S(1)} %shard_map.489), channel_id=1, source_target_pairs={{0,1},{1,0},{2,3},{3,2},{4,5},{5,4},{6,7},{7,6},{8,9},{9,8},{10,11... | collective-permute-start | bytes 12296 | tf_op jit(solution)/shard_map/ppermute | solution.py:116
  257.5 4.1 %collective-permute-start.57 = (f32[8,128]{1,0:T(8,128)S(1)}, f32[8,128]{1,0:T(8,128)S(1)}, u32[]{:S(2)}, u32[]{:S(2)}) collective-permute-start(f32[8,128]{1,0:T(8,128)S(1)} %add.29), channel_id=1, source_target_pairs={{0,8},{4,12},{8,0},{12,4},{16,24},{20,28},{24,16},{28,20},{1,9},{5... | collective-permute-start | bytes 12296 | tf_op jit(solution)/shard_map/ppermute | solution.py:116
  260.0 3.6 %collective-permute-start.55 = (f32[8,128]{1,0:T(8,128)S(1)}, f32[8,128]{1,0:T(8,128)S(1)}, u32[]{:S(2)}, u32[]{:S(2)}) collective-permute-start(f32[8,128]{1,0:T(8,128)S(1)} %add.28.partial_ref), channel_id=1, source_target_pairs={{0,2},{1,3},{2,0},{3,1},{4,6},{5,7},{6,4},{7,5},{8,10},{9,11},{10,... | collective-permute-start | bytes 12296 | tf_op jit(solution)/shard_map/ppermute | solution.py:116
  261.6 8.1 %collective-permute-start.58 = (f32[8,128]{1,0:T(8,128)S(1)}, f32[8,128]{1,0:T(8,128)S(1)}, u32[]{:S(2)}, u32[]{:S(2)}) collective-permute-start(f32[8,128]{1,0:T(8,128)S(1)} %add.30), channel_id=1, source_target_pairs={{0,16},{4,20},{8,24},{12,28},{16,0},{20,4},{24,8},{28,12},{1,17},{... | collective-permute-start | bytes 12296 | tf_op jit(solution)/shard_map/ppermute | solution.py:116
  (33 other events, 227.9 us)
